TPU v7x, 256 devices: a whole 4x4x8 slice. The times are simulated.
256 devices in a mesh: ctx: 32 (over z, x_lo, core), head: 8 (over x_hi, y).
Axes of the slice: x: 4 (x_hi: 2, x_lo: 2; x = x_hi * 2 + x_lo), y: 4, z: 8, core: 2. Of those that a mesh axis runs over, the one named last changes fastest.
Arguments:
- queries: bfloat16 [128, 128, 192], P('ctx', 'head'), may hold values from -200 to 200
- out_grad: bfloat16 [128, 128, 128], P('ctx', 'head'), may hold values from -6 to 6
- kv_up: bfloat16 [128, 512, 256], P('head'), may hold values from -0.25 to 0.25
- latent_cache: bfloat16 [32768, 576], P('ctx'), may hold values from -12 to 12
- token_ratio: float32 [128], P('ctx'), may hold values from -4 to 4
- pair_lens: int32 [4], replicated, may hold values from 1 to 64, 128 in all
- prompt_len: int32 [1], replicated, may hold values from 16384 to 32768
Outputs:
- query_grad: bfloat16 [128, 128, 192], P('ctx', 'head')
- cache_grad: bfloat16 [32768, 576], P(('ctx', 'head'))
All inputs are finite; a program needn't handle non-finite values.
Results may differ from a plain program's by a relative error of at most 0.029.
Values may be sent and summed in bfloat16 or wider, within the bound.
No kernel may reach another device: no remote copies, remote signals or barrier semaphores. Data moves between devices by JAX's collectives and lax.ppermute only.
A program may use at most 128 MiB of HBM per device.

v0:
```python
import functools

import jax
import jax.numpy as jnp
from jax import lax
from jax.experimental import pallas as pl
from jax.experimental.pallas import tpu as pltpu
from jax.sharding import PartitionSpec as P

BETA = 0.1
LOSS_SCALE = 2048.0
LOG2E = 1.4426950408889634
NEVER = -1e30
FLOOR = -1e29
F32 = jnp.float32
BF16 = jnp.bfloat16
CHUNK = 128
VMEM_BYTES = 40 * 1024 * 1024


def segment_table(rows, pair_lens):
    bounds = jnp.cumsum(pair_lens)
    segment = jnp.sum((rows[:, None] >= bounds[None, :]).astype(jnp.int32), axis=1)
    labels = jnp.arange(pair_lens.shape[0], dtype=jnp.int32)
    return (segment[:, None] == labels[None, :]).astype(F32)


def pair_gains(ratios):
    margin = BETA * (ratios[0::2] - ratios[1::2])
    weight = LOSS_SCALE * BETA * jax.nn.sigmoid(-margin)
    return jnp.stack([-weight, weight], axis=1).reshape(-1)


def row_gains(token_ratio, pair_lens):
    table = segment_table(jnp.arange(token_ratio.shape[0], dtype=jnp.int32), pair_lens)
    ratios = jnp.sum(table * token_ratio[:, None], axis=0)
    return jnp.sum(table * pair_gains(ratios)[None, :], axis=1)


def permute(x, axis, to):
    return lax.ppermute(x, axis, [(i, to(i)) for i in range(lax.axis_size(axis))])


def in_order(mine, theirs, second, axis):
    return jnp.where(
        second,
        jnp.concatenate([theirs, mine], axis),
        jnp.concatenate([mine, theirs], axis),
    )


def pick(x, index, axis):
    return lax.dynamic_index_in_dim(x, index, axis, keepdims=False)


def join_stats(first, second):
    top = jnp.maximum(first[0], second[0])
    one = jnp.exp2(first[0] - top)
    two = jnp.exp2(second[0] - top)
    return jnp.stack([top, one * first[1] + two * second[1], one * first[2] + two * second[2]])


def against(x, y):
    return lax.dot_general(x, y, (((1,), (1,)), ((), ())), preferred_element_type=F32)


def attend_kernel(
    score_scale,
    where_ref,
    rows_ref,
    kv_ref,
    own_ref,
    other_ref,
    query_ref,
    grad_ref,
    expo_ref,
    spread_ref,
    stats_ref,
    scores,
    dprod,
):
    rows, d_nope = rows_ref.shape[1], kv_ref.shape[2] // 2
    d_lat = kv_ref.shape[1]
    d_rope = query_ref.shape[1] - d_lat
    keys = own_ref.shape[0]
    width = query_ref.shape[0]
    for j in range(rows_ref.shape[0]):
        at = slice(j * rows, (j + 1) * rows)
        lat = against(rows_ref[j, :, :d_nope], kv_ref[j, :, :d_nope])
        query_ref[at, :d_lat] = lat.astype(BF16)
        query_ref[at, d_lat:] = rows_ref[j, :, 2 * d_nope : 2 * d_nope + d_rope]
        lat = against(rows_ref[j, :, d_nope : 2 * d_nope], kv_ref[j, :, d_nope:])
        grad_ref[at, :] = lat.astype(BF16)
    scores[:keys] = against(own_ref[...], query_ref[...])
    scores[keys:] = against(other_ref[...], query_ref[...])
    dprod[:keys] = against(own_ref[:, :d_lat], grad_ref[...])
    dprod[keys:] = against(other_ref[:, :d_lat], grad_ref[...])
    steps = 2 * keys // CHUNK

    def fold(x, join):
        return join(x.reshape(CHUNK // 8, 8, width), axis=0)

    def highest(i, top):
        at = pl.ds(pl.multiple_of(i * CHUNK, CHUNK), CHUNK)
        first = jnp.where(i * CHUNK < keys, where_ref[1], where_ref[2] - keys) + i * CHUNK
        key = first + lax.broadcasted_iota(jnp.int32, (CHUNK, width), 0)
        value = jnp.where(key < where_ref[3], scores[at, :] * score_scale, NEVER)
        scores[at, :] = value
        return jnp.maximum(top, fold(value, jnp.max))

    top = lax.fori_loop(0, steps, highest, jnp.full((8, width), FLOOR, F32), unroll=2)
    top = jnp.max(top, axis=0, keepdims=True)

    def sums(i, so_far):
        at = pl.ds(pl.multiple_of(i * CHUNK, CHUNK), CHUNK)
        value = jnp.exp2(scores[at, :] - top)
        scores[at, :] = value
        expo_ref[at, :] = value.astype(BF16)
        return (
            so_far[0] + fold(value, jnp.sum),
            so_far[1] + fold(value * dprod[at, :], jnp.sum),
        )

    zero = jnp.zeros((8, width), F32)
    mass, dsum = lax.fori_loop(0, steps, sums, (zero, zero), unroll=2)
    mass = jnp.sum(mass, axis=0, keepdims=True)
    dsum = jnp.sum(dsum, axis=0, keepdims=True)
    centre = dsum / jnp.maximum(mass, 1e-30)

    def spreads(i, carry):
        at = pl.ds(pl.multiple_of(i * CHUNK, CHUNK), CHUNK)
        spread_ref[at, :] = (scores[at, :] * (dprod[at, :] - centre)).astype(BF16)
        return carry

    lax.fori_loop(0, steps, spreads, 0, unroll=2)
    stats_ref[0:1] = top
    stats_ref[1:2] = mass
    stats_ref[2:3] = dsum


def attend(where, everything, kv_up, own, other, score_scale):
    half, rows, packed = everything.shape
    d_lat = kv_up.shape[1]
    keys, c_width = own.shape
    total = half * rows
    width = 2 * rows
    whole = lambda p, w: (0, 0)
    column = lambda p, w: (0, p)
    return pl.pallas_call(
        functools.partial(attend_kernel, score_scale),
        out_shape=(
            jax.ShapeDtypeStruct((total, c_width), BF16),
            jax.ShapeDtypeStruct((total, d_lat), BF16),
            jax.ShapeDtypeStruct((2 * keys, total), BF16),
            jax.ShapeDtypeStruct((2 * keys, total), BF16),
            jax.ShapeDtypeStruct((3, total), F32),
        ),
        grid_spec=pltpu.PrefetchScalarGridSpec(
            num_scalar_prefetch=1,
            grid=(half // 2,),
            in_specs=[
                pl.BlockSpec((2, rows, packed), lambda p, w: (p, 0, 0)),
                pl.BlockSpec((2,) + kv_up.shape[1:], lambda p, w: (w[0] * (half // 2) + p, 0, 0)),
                pl.BlockSpec((keys, c_width), whole),
                pl.BlockSpec((keys, c_width), whole),
            ],
            out_specs=[
                pl.BlockSpec((width, c_width), lambda p, w: (p, 0)),
                pl.BlockSpec((width, d_lat), lambda p, w: (p, 0)),
                pl.BlockSpec((2 * keys, width), column),
                pl.BlockSpec((2 * keys, width), column),
                pl.BlockSpec((3, width), column),
            ],
            scratch_shapes=[
                pltpu.VMEM((2 * keys, width), F32),
                pltpu.VMEM((2 * keys, width), F32),
            ],
        ),
        compiler_params=pltpu.CompilerParams(vmem_limit_bytes=VMEM_BYTES),
        cost_estimate=pl.CostEstimate(
            flops=2 * 2 * keys * total * (c_width + d_lat),
            bytes_accessed=8 * keys * total,
            transcendentals=2 * keys * total,
        ),
    )(where, everything, kv_up, own, other)


def project_kernel(where_ref, cache_ref, spread_ref, expo_ref, kv_ref, by_spread_ref, by_expo_ref):
    d_lat = kv_ref.shape[1]
    d_nope = kv_ref.shape[2] // 2
    rows = spread_ref.shape[1] // kv_ref.shape[0]
    for terms_ref, out_ref in ((spread_ref, by_spread_ref), (expo_ref, by_expo_ref)):
        full = jnp.dot(cache_ref[...], terms_ref[...], preferred_element_type=F32)
        for j in range(kv_ref.shape[0]):
            at = slice(j * rows, (j + 1) * rows)
            lat = full[:d_lat, at].astype(BF16)
            out_ref[at, :d_nope] = lax.dot_general(
                lat,
                kv_ref[j, :, :d_nope],
                (((0,), (0,)), ((), ())),
                preferred_element_type=F32,
            )
            out_ref[at, d_nope:] = full[d_lat:, at].T


def project(where, cache_t, spread, expo, kv_up, half, q_width):
    c_width, keys = cache_t.shape
    total = spread.shape[1]
    width = 2 * total // half
    column = pl.BlockSpec((keys, width), lambda p, w: (0, p))
    result = pl.BlockSpec((width, q_width), lambda p, w: (p, 0))
    return pl.pallas_call(
        project_kernel,
        out_shape=(jax.ShapeDtypeStruct((total, q_width), F32),) * 2,
        grid_spec=pltpu.PrefetchScalarGridSpec(
            num_scalar_prefetch=1,
            grid=(half // 2,),
            in_specs=[
                pl.BlockSpec((c_width, keys), lambda p, w: (0, 0)),
                column,
                column,
                pl.BlockSpec((2,) + kv_up.shape[1:], lambda p, w: (w[0] * (half // 2) + p, 0, 0)),
            ],
            out_specs=[result, result],
        ),
        compiler_params=pltpu.CompilerParams(vmem_limit_bytes=VMEM_BYTES),
        cost_estimate=pl.CostEstimate(
            flops=4 * keys * total * c_width, bytes_accessed=4 * keys * total, transcendentals=0
        ),
    )(where, cache_t, spread, expo, kv_up)


def weigh_kernel(
    scale,
    joined_ref,
    own_ref,
    gains_ref,
    query_ref,
    grad_ref,
    by_spread_ref,
    by_expo_ref,
    spread_ref,
    expo_ref,
    dq_ref,
    with_spread_ref,
    with_expo_ref,
    out_ref,
):
    total = query_ref.shape[0]
    d_lat = grad_ref.shape[1]

    @pl.when(pl.program_id(0) == 0)
    def _():
        tops = [joined_ref[k, 0:1] for k in range(joined_ref.shape[0])]
        top = functools.reduce(jnp.maximum, tops)
        mass = jnp.zeros_like(top)
        dsum = jnp.zeros_like(top)
        for k in range(joined_ref.shape[0]):
            part = jnp.exp2(tops[k] - top)
            mass = mass + part * joined_ref[k, 1:2]
            dsum = dsum + part * joined_ref[k, 2:3]
        centre = own_ref[2:3] / jnp.maximum(own_ref[1:2], 1e-30)
        factor = gains_ref[...] * jnp.exp2(own_ref[0:1] - top) / mass
        shift = dsum / mass - centre
        sublane = lax.broadcasted_iota(jnp.int32, (8, total), 0)
        both = jnp.where(sublane == 0, factor, shift).T
        factor = both[:, 0:1]
        shift = both[:, 1:2]
        scaled = scale * factor
        dq = (scaled * (by_spread_ref[...] - shift * by_expo_ref[...])).astype(BF16)
        blocks, half, size = dq_ref.shape[0], dq_ref.shape[1], dq_ref.shape[2]
        for h in range(half):
            for b in range(blocks):
                first = (h * blocks + b) * size
                dq_ref[b, h] = dq[first : first + size]
        query = scaled * query_ref[...].astype(F32)
        with_spread_ref[...] = query.astype(BF16)
        moved = shift * query
        with_expo_ref[:, :d_lat] = (
            factor * grad_ref[...].astype(F32) - moved[:, :d_lat]
        ).astype(BF16)
        with_expo_ref[:, d_lat:] = (-moved[:, d_lat:]).astype(BF16)

    out = jnp.dot(spread_ref[...], with_spread_ref[...], preferred_element_type=F32)
    out = out + jnp.dot(expo_ref[...], with_expo_ref[...], preferred_element_type=F32)
    out_ref[...] = out.astype(BF16)


def weigh(joined, stats, gains, query, grad, by_spread, by_expo, spread, expo, scale, blocks, half):
    keys, total = spread.shape[0] // 2, spread.shape[1]
    c_width = query.shape[1]
    q_width = by_spread.shape[1]
    size = total // (half * blocks)
    tile = keys // 2
    whole = lambda x: pl.BlockSpec(x.shape, lambda i: (0,) * len(x.shape))
    dq = jax.ShapeDtypeStruct((blocks, half, size, q_width), BF16)
    weight = jax.ShapeDtypeStruct((total, c_width), BF16)
    second = pl.BlockSpec((tile, total), lambda i: (i + 2, 0))
    return pl.pallas_call(
        functools.partial(weigh_kernel, scale),
        out_shape=(dq, weight, weight, jax.ShapeDtypeStruct((keys, c_width), BF16)),
        grid=(2,),
        in_specs=[whole(x) for x in (joined, stats, gains, query, grad, by_spread, by_expo)]
        + [second, second],
        out_specs=[
            whole(dq),
            whole(weight),
            whole(weight),
            pl.BlockSpec((tile, c_width), lambda i: (i, 0)),
        ],
        compiler_params=pltpu.CompilerParams(vmem_limit_bytes=VMEM_BYTES),
        cost_estimate=pl.CostEstimate(
            flops=4 * keys * total * c_width, bytes_accessed=4 * keys * total, transcendentals=0
        ),
    )(joined, stats, gains, query, grad, by_spread, by_expo, spread, expo)


def cache_kernel(spread_ref, expo_ref, with_spread_ref, with_expo_ref, out_ref):
    out = jnp.dot(spread_ref[...], with_spread_ref[...], preferred_element_type=F32)
    out_ref[...] = out + jnp.dot(expo_ref[...], with_expo_ref[...], preferred_element_type=F32)


def cache_terms(spread, expo, with_spread, with_expo):
    keys, total = spread.shape[0] // 2, spread.shape[1]
    c_width = with_spread.shape[1]
    tile = keys // 2
    first = pl.BlockSpec((tile, total), lambda i: (i, 0))
    weight = pl.BlockSpec((total, c_width), lambda i: (0, 0))
    return pl.pallas_call(
        cache_kernel,
        out_shape=jax.ShapeDtypeStruct((keys, c_width), F32),
        grid=(2,),
        in_specs=[first, first, weight, weight],
        out_specs=pl.BlockSpec((tile, c_width), lambda i: (i, 0)),
        compiler_params=pltpu.CompilerParams(vmem_limit_bytes=VMEM_BYTES),
        cost_estimate=pl.CostEstimate(
            flops=4 * keys * total * c_width, bytes_accessed=4 * keys * total, transcendentals=0
        ),
    )(spread, expo, with_spread, with_expo)


def per_device(queries, out_grad, kv_up, latent_cache, token_ratio, pair_lens, prompt_len):
    ctx_index = lax.axis_index("ctx")
    head_index = lax.axis_index("head")
    core = ctx_index % 2
    x_lo = (ctx_index // 2) % 2
    z = ctx_index // 4
    nz = lax.axis_size("ctx") // 4
    ny = lax.axis_size("head") // 2
    y = head_index % ny
    x_hi = head_index // ny
    other_core = lambda i: i ^ 1
    other_x_lo = lambda i: i ^ 2
    z_groups = [[4 * k + j for k in range(nz)] for j in range(4)]

    q_dev, heads, q_width = queries.shape
    p_dev, c_width = latent_cache.shape
    d_lat = kv_up.shape[1]
    d_rope = c_width - d_lat
    d_nope = q_width - d_rope
    half = heads // 2
    rows = q_dev * 4 * nz
    scale = q_width ** (-0.5)

    other_cache = permute(latent_cache, "ctx", other_core)

    high = lax.reduce_precision(token_ratio, 8, 7)
    middle = lax.reduce_precision(token_ratio - high, 8, 7)
    low = token_ratio - high - middle
    terms = jnp.stack([high, middle, low], axis=1).astype(BF16)
    terms = jnp.broadcast_to(terms[:, None, :], (q_dev, heads, 3))
    own = jnp.concatenate(
        [queries[:, :, :d_nope], out_grad, queries[:, :, d_nope:], terms], axis=2
    )
    own = jnp.transpose(own, (1, 0, 2)).reshape(2, half, q_dev, -1)
    block = jnp.concatenate(
        [pick(own, core, 0), permute(pick(own, 1 - core, 0), "ctx", other_core)], 1
    )
    block = in_order(block, permute(block, "ctx", other_x_lo), x_lo == 1, 1)
    up = down = block
    ring = [block] + [None] * (nz - 1)
    for k in range(1, nz // 2 + 1):
        up = permute(up, "ctx", lambda i: (i + 4) % (4 * nz))
        ring[nz - k] = up
        if k < nz // 2:
            down = permute(down, "ctx", lambda i: (i - 4) % (4 * nz))
            ring[k] = down
    ring = jnp.stack(ring, axis=1)
    ring = jnp.concatenate([ring, ring], axis=1)
    everything = lax.dynamic_slice_in_dim(ring, (nz - z) % nz, nz, 1)
    everything = everything.reshape(half, rows, -1)

    ratio = jnp.sum(everything[0, :, -3:].astype(F32), axis=1).reshape(nz, 2, 2, q_dev)
    ratio = jnp.where(core == 1, ratio[:, :, ::-1], ratio).reshape(rows)
    gains = row_gains(ratio, pair_lens).reshape(nz, 2, 2, q_dev)
    gains = jnp.where(core == 1, gains[:, :, ::-1], gains).reshape(1, rows)
    gains = jnp.tile(gains, (1, half))

    where = jnp.stack(
        [core, ctx_index * p_dev, (ctx_index ^ 1) * p_dev, prompt_len[0]]
    ).astype(jnp.int32)
    query, grad, expo, spread, stats = attend(
        where, everything, kv_up, latent_cache, other_cache, scale * LOG2E
    )
    cache_t = jnp.concatenate([latent_cache, other_cache], axis=0).T
    pair = permute(stats, "ctx", other_x_lo)
    by_spread, by_expo = project(where, cache_t, spread, expo, kv_up, half, q_width)
    pair, by_spread, by_expo = lax.optimization_barrier((pair, by_spread, by_expo))
    joined = join_stats(stats, pair)
    joined = lax.all_to_all(
        jnp.broadcast_to(joined[None], (nz,) + joined.shape),
        "ctx",
        0,
        0,
        axis_index_groups=z_groups,
    )
    dq, with_spread, with_expo, for_other = weigh(
        joined, stats, gains, query, grad, by_spread, by_expo, spread, expo, scale, nz, half
    )
    from_other = permute(for_other, "ctx", other_core)
    partial = cache_terms(spread, expo, with_spread, with_expo)

    partial = partial.reshape(2, ny, p_dev // (2 * ny), c_width)
    from_other = from_other.reshape(partial.shape)

    def for_y(k):
        at = (y + k) % ny
        return pick(partial, at, 1) + pick(from_other, at, 1).astype(F32)

    blocks = [for_y(k).astype(BF16) for k in range(1, ny)]
    blocks, dq = lax.optimization_barrier((blocks, dq))
    arrived = [
        permute(blocks[k - 1], "head", lambda i, k=k: (i // ny) * ny + (i + k) % ny)
        for k in range(1, ny)
    ]

    dq = lax.all_to_all(dq, "ctx", 0, 0, axis_index_groups=z_groups)
    dq = jnp.sum(dq.astype(F32), axis=0).reshape(half, 2, 2 * q_dev, q_width)
    from_pair = permute(pick(dq, 1 - x_lo, 1).astype(BF16), "ctx", other_x_lo)
    dq = (pick(dq, x_lo, 1) + from_pair.astype(F32)).astype(BF16)
    theirs = permute(dq[:, q_dev:], "ctx", other_core)
    query_grad = jnp.transpose(in_order(dq[:, :q_dev], theirs, core == 1, 0), (1, 0, 2))

    total = for_y(0)
    for part in arrived:
        total = total + part.astype(F32)
    across = permute(
        pick(total, 1 - x_hi, 0).astype(BF16), "head", lambda i: (i + ny) % (2 * ny)
    )
    cache_grad = (pick(total, x_hi, 0) + across.astype(F32)).astype(BF16)
    return (query_grad, cache_grad)


def solution(mesh):
    placed = (
        P("ctx", "head", None),
        P("ctx", "head", None),
        P("head", None, None),
        P("ctx", None),
        P("ctx"),
        P(),
        P(),
    )
    return jax.shard_map(
        per_device,
        mesh=mesh,
        in_specs=placed,
        out_specs=(P("ctx", "head", None), P(("ctx", "head"), None)),
        check_vma=False,
    )
```

profile of v0, /device:TPU:1, one launch (start us, length us, event | category | flops | bytes accessed | tf_op | source)
XLA Modules:
  0.0 162.9 jit_solution(15335326653251318367)
XLA Ops:
  0.6 0.7 slice.41
  1.4 0.7 slice.42
  2.1 0.7 fusion.11
  2.9 0.8 maximum_bitcast_fusion.1
  3.7 3.3 %collective-permute-start = (bf16[8,4,323]{2,1,0:T(4,128)(2,1)S(1)}, bf16[8,4,323]{2,1,0:T(4,128)(2,1)S(1)}, u32[]{:S(2)}, u32[]{:S(2)}) collective-permute-start(bf16[8,4,323]{2,1,0:T(4,128)(2,1)S(1)} %bitcast.117), channel_id=1, source_target_pairs={{0,8},{8,0},{16,24},{24,16},{32,40},{40,32},{48,56},{56,48},{64,72... | collective-permute-start | bytes 62024 | tf_op jit(solution)/shard_map/ppermute | solution.py:41
  7.1 0.8 reduce-window.8
  8.9 2.4 %copy.117.own_ref = bf16[1024,576]{1,0:T(8,128)(2,1)} copy(bf16[1024,576]{0,1:T(8,128)(2,1)} %param.10) | data formatting | bytes 2359296 | tf_op args[3]
  11.4 0.4 collective-permute-done.1
  11.9 4.7 %collective-permute-start.2 = (bf16[8,16,323]{2,1,0:T(8,128)(2,1)S(1)}, bf16[8,16,323]{2,1,0:T(8,128)(2,1)S(1)}, u32[]{:S(2)}, u32[]{:S(2)}) collective-permute-start(bf16[8,16,323]{2,1,0:T(8,128)(2,1)S(1)} %maximum_select_fusion.1), channel_id=1, source_target_pairs={{0,224},{8,232},{16,240},{24,248},{32,0},{40,8},{48,16},{56,24},{6... | collective-permute-start | bytes 248072 | tf_op jit(solution)/shard_map/ppermute | solution.py:41
  16.7 1.6 collective-permute-done.2
  18.2 3.0 %collective-permute-start.3 = (bf16[8,16,323]{2,1,0:T(8,128)(2,1)S(1)}, bf16[8,16,323]{2,1,0:T(8,128)(2,1)S(1)}, u32[]{:S(2)}, u32[]{:S(2)}) collective-permute-start(bf16[8,16,323]{2,1,0:T(8,128)(2,1)S(1)} %collective-permute-done.2), channel_id=1, source_target_pairs={{0,224},{8,232},{16,240},{24,248},{32,0},{40,8},{48,16},{56,24},{6... | collective-permute-start | bytes 248072 | tf_op jit(solution)/shard_map/ppermute | solution.py:41
  21.3 1.6 collective-permute-done.3
  22.9 3.0 %collective-permute-start.4 = (bf16[8,16,323]{2,1,0:T(8,128)(2,1)S(1)}, bf16[8,16,323]{2,1,0:T(8,128)(2,1)S(1)}, u32[]{:S(2)}, u32[]{:S(2)}) collective-permute-start(bf16[8,16,323]{2,1,0:T(8,128)(2,1)S(1)} %collective-permute-done.3), channel_id=1, source_target_pairs={{0,224},{8,232},{16,240},{24,248},{32,0},{40,8},{48,16},{56,24},{6... | collective-permute-start | bytes 248072 | tf_op jit(solution)/shard_map/ppermute | solution.py:41
  26.0 4.7 %collective-permute-done.7 = bf16[8,16,323]{2,1,0:T(8,128)(2,1)S(1)} collective-permute-done((bf16[8,16,323]{2,1,0:T(8,128)(2,1)S(1)}, bf16[8,16,323]{2,1,0:T(8,128)(2,1)S(1)}, u32[]{:S(2)}, u32[]{:S(2)}) %collective-permute-start.7) | collective-permute-done | bytes 82720 | tf_op jit(solution)/shard_map/ppermute | solution.py:41
  30.6 4.8 %collective-permute-done.8 = bf16[8,16,323]{2,1,0:T(8,128)(2,1)S(1)} collective-permute-done((bf16[8,16,323]{2,1,0:T(8,128)(2,1)S(1)}, bf16[8,16,323]{2,1,0:T(8,128)(2,1)S(1)}, u32[]{:S(2)}, u32[]{:S(2)}) %collective-permute-start.8) | collective-permute-done | bytes 82720 | tf_op jit(solution)/shard_map/ppermute | solution.py:41
  37.2 1.0 copy-done.17
  38.3 0.7 copy.118.other_ref
  39.0 1.3 copy-done.5
  40.3 14.6 %shard_map.86 = (bf16[1024,576]{1,0:T(8,128)(2,1)S(1)}, bf16[1024,512]{1,0:T(8,128)(2,1)S(1)}, bf16[2048,1024]{1,0:T(8,128)(2,1)S(1)}, bf16[2048,1024]{1,0:T(8,128)(2,1)S(1)}, f32[3,1024]{1,0:T(4,128)S(1)}) custom-call(s32[4]{0:T(128)S(1)} %pad_add_fusion.where_ref, bf16[8,128,323]{2,1,0:T(8,128)(2,1)S(1)} %bitcast.104, bf16[16,512,256]{2,1,0:T(8,128)(2,1)} %kv_ref.3, ...), custom_call_target="tpu_custom_call" | custom-call | flops 4563402752 | bytes 8388608 | tf_op jit(solution)/shard_map/pallas_call | solution.py:149
  55.0 1.0 copy-done.10
  56.0 1.4 collective-permute-start.10
  57.6 0.3 copy-done
  57.9 14.7 %shard_map.87 = (f32[1024,192]{1,0:T(8,128)S(1)}, f32[1024,192]{1,0:T(8,128)S(1)}) custom-call(s32[4]{0:T(128)S(1)} %pad_add_fusion.where_ref, bf16[576,2048]{1,0:T(8,128)(2,1)S(1)} %maximum_bitcast_fusion.cache_ref, bf16[2048,1024]{1,0:T(8,128)(2,1)S(1)} %get-tuple-element.20.spread_ref, bf16[2048,1024]{1,0:T(8,128)(2,1)S(1)} %get-tuple-element.21.expo_ref, ...), custom_call_target="tpu_custom_call" | custom-call | flops 4831838208 | bytes 8388608 | tf_op jit(solution)/shard_map/pallas_call | solution.py:212
  72.7 2.0 %copy-done.2 = bf16[2048,1024]{1,0:T(8,128)(2,1)} copy-done((bf16[2048,1024]{1,0:T(8,128)(2,1)}, bf16[2048,1024]{1,0:T(8,128)(2,1)S(1)}, u32[]{:S(2)}) %copy-start.2) | copy-done | bytes 4194328
  74.7 1.0 copy-done.12
  75.7 1.0 copy-done.14
  76.8 0.7 broadcast_in_dim.5
  77.4 3.4 %all-to-all-start = ((f32[8,3,1024]{2,1,0:T(4,128)}), f32[8,3,1024]{2,1,0:T(4,128)S(1)}, u32[]{:S(2)}, u32[]{:S(2)}) async-start(f32[8,3,1024]{2,1,0:T(4,128)} %broadcast_in_dim.5), calls=%async_computation | async-start | bytes 262144 | tf_op jit(solution)/shard_map/all_to_all | solution.py:410
  81.0 7.7 %all-to-all-done.joined_ref = f32[8,3,1024]{2,1,0:T(4,128)S(1)} async-done(((f32[8,3,1024]{2,1,0:T(4,128)}), f32[8,3,1024]{2,1,0:T(4,128)S(1)}, u32[]{:S(2)}, u32[]{:S(2)}) %all-to-all-start) | async-done | bytes 98336 | tf_op jit(solution)/shard_map/all_to_all | solution.py:410
  88.7 2.2 %copy-done.3 = bf16[2048,1024]{1,0:T(8,128)(2,1)S(1)} copy-done((bf16[2048,1024]{1,0:T(8,128)(2,1)S(1)}, bf16[2048,1024]{1,0:T(8,128)(2,1)}, u32[]{:S(2)}) %copy-start.3) | copy-done | bytes 4194328
  90.9 1.2 copy-done.11
  92.1 1.2 copy-done.13
  93.3 1.2 copy-done.15
  94.5 6.2 %shard_map.88 = (bf16[8,8,16,192]{3,2,1,0:T(8,128)(2,1)}, bf16[1024,576]{1,0:T(8,128)(2,1)S(1)}, bf16[1024,576]{1,0:T(8,128)(2,1)S(1)}, bf16[1024,576]{1,0:T(8,128)(2,1)S(1)}) custom-call(f32[8,3,1024]{2,1,0:T(4,128)S(1)} %all-to-all-done.joined_ref, f32[3,1024]{1,0:T(4,128)S(1)} %get-tuple-element.22.own_ref, f32[1,1024]{1,0:T(1,128)S(1)} %bitcast.105, ...), custom_call_target="tpu_custom_call" | custom-call | flops 2415919104 | bytes 4194304 | tf_op jit(solution)/shard_map/pallas_call | solution.py:299
  100.7 1.1 copy-done.6
  101.8 1.1 copy-done.8
  102.9 1.4 copy.121
  104.3 7.4 %collective-permute-start.11 = (bf16[1024,576]{0,1:T(8,128)(2,1)}, bf16[1024,576]{0,1:T(8,128)(2,1)}, u32[]{:S(2)}, u32[]{:S(2)}) collective-permute-start(bf16[1024,576]{0,1:T(8,128)(2,1)} %copy.121), channel_id=1, source_target_pairs={{0,8},{8,0},{16,24},{24,16},{32,40},{40,32},{48,56},{56,48},{64,72... | collective-permute-start | bytes 3538952 | tf_op jit(solution)/shard_map/ppermute | solution.py:41
  111.7 2.2 %copy-done.1 = bf16[2048,1024]{1,0:T(8,128)(2,1)S(1)} copy-done((bf16[2048,1024]{1,0:T(8,128)(2,1)S(1)}, bf16[2048,1024]{1,0:T(8,128)(2,1)}, u32[]{:S(2)}) %copy-start.1) | copy-done | bytes 4194328
  113.8 2.2 %copy-done.4 = bf16[2048,1024]{1,0:T(8,128)(2,1)S(1)} copy-done((bf16[2048,1024]{1,0:T(8,128)(2,1)S(1)}, bf16[2048,1024]{1,0:T(8,128)(2,1)}, u32[]{:S(2)}) %copy-start.4) | copy-done | bytes 4194328
  116.0 1.3 copy-done.9
  117.3 3.6 %shard_map.89 = f32[1024,576]{1,0:T(8,128)S(1)} custom-call(bf16[2048,1024]{1,0:T(8,128)(2,1)S(1)} %copy-done.4, bf16[2048,1024]{1,0:T(8,128)(2,1)S(1)} %copy-done.1, bf16[1024,576]{1,0:T(8,128)(2,1)S(1)} %copy-done.7, bf16[1024,576]{1,0:T(8,128)(2,1)S(1)} %copy-done.9), custom_call_target="tpu_custom_call" | custom-call | flops 2415919104 | bytes 4194304 | tf_op jit(solution)/shard_map/pallas_call | solution.py:329
  121.1 1.1 copy.135
  122.2 0.2 copy.131
  122.5 0.2 copy.133
  122.7 2.7 %reshape.191 = bf16[2,4,128,576]{2,1,0,3:T(4,128)(2,1)S(1)} reshape(bf16[1024,576]{0,1:T(8,128)(2,1)} %collective-permute-done.11) | data formatting | bytes 2359296 | tf_op jit(solution)/shard_map/reshape | solution.py:424
  125.4 3.3 %constant_dynamic-slice_fusion = (bf16[2,1,128,576]{2,1,0,3:T(2,128)(2,1)}, bf16[2,1,128,576]{2,1,0,3:T(2,128)(2,1)S(1)}, bf16[2,1,128,576]{2,1,0,3:T(2,128)(2,1)S(1)}, bf16[2,1,128,576]{2,1,0,3:T(2,128)(2,1)S(1)}) fusion(bf16[2,4,128,576]{2,1,0,3:T(4,128)(2,1)S(1)} %reshape.191, s32[]{:T(128)S(6)} %select_n.153, s32[]{:T(128)S(6)} %select_n.148, ...), kind=kLoop, calls=%fused_computation.53 | loop fusion | bytes 2359312 | tf_op jit(solution)/shard_map/jit(dynamic_index_in_dim)/dynamic_slice | solution.py:53
  128.7 0.8 fusion.4
  129.5 0.9 fusion.2
  130.3 1.3 collective-permute-start.14
  131.6 2.6 %collective-permute-start.15 = (bf16[2,128,576]{1,2,0:T(8,128)(2,1)S(1)}, bf16[2,128,576]{1,2,0:T(8,128)(2,1)S(1)}, u32[]{:S(2)}, u32[]{:S(2)}) collective-permute-start(bf16[2,128,576]{1,2,0:T(8,128)(2,1)S(1)} %get-tuple-element.36), channel_id=1, source_target_pairs={{0,2},{1,3},{2,0},{3,1},{4,6},{5,7},{6,4},{7,5},{8,10},{9,11},{10,... | collective-permute-start | bytes 884744 | tf_op jit(solution)/shard_map/ppermute | solution.py:41
  134.2 1.1 collective-permute-start.16
  135.3 3.5 %all-to-all-start.1 = ((bf16[8,8,16,192]{3,2,1,0:T(8,128)(2,1)}), bf16[8,8,16,192]{3,2,1,0:T(8,128)(2,1)S(1)}, u32[]{:S(2)}, u32[]{:S(2)}) async-start(bf16[8,8,16,192]{3,2,1,0:T(8,128)(2,1)} %get-tuple-element.34), calls=%async_computation.1 | async-start | bytes 1048576 | tf_op jit(solution)/shard_map/all_to_all | solution.py:437
  138.9 0.2 copy.138
  139.1 1.4 collective-permute-done.14
  140.5 7.4 %collective-permute-done.15 = bf16[2,128,576]{1,2,0:T(8,128)(2,1)S(1)} collective-permute-done((bf16[2,128,576]{1,2,0:T(8,128)(2,1)S(1)}, bf16[2,128,576]{1,2,0:T(8,128)(2,1)S(1)}, u32[]{:S(2)}, u32[]{:S(2)}) %collective-permute-start.15) | collective-permute-done | bytes 294944 | tf_op jit(solution)/shard_map/ppermute | solution.py:41
  148.0 1.1 fusion.1
  149.1 2.6 %collective-permute-start.17 = (bf16[128,576]{0,1:T(8,128)(2,1)S(1)}, bf16[128,576]{0,1:T(8,128)(2,1)S(1)}, u32[]{:S(2)}, u32[]{:S(2)}) collective-permute-start(bf16[128,576]{0,1:T(8,128)(2,1)S(1)} %fusion.6), channel_id=1, source_target_pairs={{0,4},{1,5},{2,6},{3,7},{4,0},{5,1},{6,2},{7,3},{8,12},{9,13},{10,... | collective-permute-start | bytes 442376 | tf_op jit(solution)/shard_map/ppermute | solution.py:41
  151.7 5.0 %all-to-all-done.1 = bf16[8,8,16,192]{3,2,1,0:T(8,128)(2,1)S(1)} async-done(((bf16[8,8,16,192]{3,2,1,0:T(8,128)(2,1)}), bf16[8,8,16,192]{3,2,1,0:T(8,128)(2,1)S(1)}, u32[]{:S(2)}, u32[]{:S(2)}) %all-to-all-start.1) | async-done | bytes 393248 | tf_op jit(solution)/shard_map/all_to_all | solution.py:437
  156.8 1.5 collective-permute-start.12
  158.3 1.3 collective-permute-done.12
  159.7 1.7 %collective-permute-start.13 = (bf16[8,4,192]{2,0,1:T(8,128)(2,1)S(1)}, bf16[8,4,192]{2,0,1:T(8,128)(2,1)S(1)}, u32[]{:S(2)}, u32[]{:S(2)}) collective-permute-start(bf16[8,4,192]{2,0,1:T(8,128)(2,1)S(1)} %get-tuple-element.52), channel_id=1, source_target_pairs={{0,8},{8,0},{16,24},{24,16},{32,40},{40,32},{48,56},{56,48},{64,72... | collective-permute-start | bytes 36872 | tf_op jit(solution)/shard_map/ppermute | solution.py:41
  161.4 0.7 fusion.5
  162.3 0.6 fusion.10
  (99 shorter events, 3.4 us)
Async XLA Ops:
  3.7 5.0 %collective-permute-start = (bf16[8,4,323]{2,1,0:T(4,128)(2,1)S(1)}, bf16[8,4,323]{2,1,0:T(4,128)(2,1)S(1)}, u32[]{:S(2)}, u32[]{:S(2)}) collective-permute-start(bf16[8,4,323]{2,1,0:T(4,128)(2,1)S(1)} %bitcast.117), channel_id=1, source_target_pairs={{0,8},{8,0},{16,24},{24,16},{32,40},{40,32},{48,56},{56,48},{64,72... | collective-permute-start | bytes 62024 | tf_op jit(solution)/shard_map/ppermute | solution.py:41
  7.0 30.2 %collective-permute-start.9 = (bf16[1024,576]{0,1:T(8,128)(2,1)}, bf16[1024,576]{0,1:T(8,128)(2,1)S(1)}, u32[]{:S(2)}, u32[]{:S(2)}) collective-permute-start(bf16[1024,576]{0,1:T(8,128)(2,1)} %param.10), channel_id=1, source_target_pairs={{0,8},{8,0},{16,24},{24,16},{32,40},{40,32},{48,56},{56,48},{64,72... | collective-permute-start | bytes 3538952 | tf_op jit(solution)/shard_map/ppermute | solution.py:41
  8.8 3.0 %collective-permute-start.1 = (bf16[8,8,323]{2,1,0:T(8,128)(2,1)S(1)}, bf16[8,8,323]{2,1,0:T(8,128)(2,1)S(1)}, u32[]{:S(2)}, u32[]{:S(2)}) collective-permute-start(bf16[8,8,323]{2,1,0:T(8,128)(2,1)S(1)} %pad_maximum_fusion), channel_id=1, source_target_pairs={{0,16},{8,24},{16,0},{24,8},{32,48},{40,56},{48,32},{56,40},{64,80... | collective-permute-start | bytes 124040 | tf_op jit(solution)/shard_map/ppermute | solution.py:41
  11.9 6.3 %collective-permute-start.2 = (bf16[8,16,323]{2,1,0:T(8,128)(2,1)S(1)}, bf16[8,16,323]{2,1,0:T(8,128)(2,1)S(1)}, u32[]{:S(2)}, u32[]{:S(2)}) collective-permute-start(bf16[8,16,323]{2,1,0:T(8,128)(2,1)S(1)} %maximum_select_fusion.1), channel_id=1, source_target_pairs={{0,224},{8,232},{16,240},{24,248},{32,0},{40,8},{48,16},{56,24},{6... | collective-permute-start | bytes 248072 | tf_op jit(solution)/shard_map/ppermute | solution.py:41
  16.6 4.7 %collective-permute-start.5 = (bf16[8,16,323]{2,1,0:T(8,128)(2,1)S(1)}, bf16[8,16,323]{2,1,0:T(8,128)(2,1)S(1)}, u32[]{:S(2)}, u32[]{:S(2)}) collective-permute-start(bf16[8,16,323]{2,1,0:T(8,128)(2,1)S(1)} %maximum_select_fusion.1), channel_id=1, source_target_pairs={{0,32},{8,40},{16,48},{24,56},{32,64},{40,72},{48,80},{56,88},{64,... | collective-permute-start | bytes 248072 | tf_op jit(solution)/shard_map/ppermute | solution.py:41
  18.2 4.7 %collective-permute-start.3 = (bf16[8,16,323]{2,1,0:T(8,128)(2,1)S(1)}, bf16[8,16,323]{2,1,0:T(8,128)(2,1)S(1)}, u32[]{:S(2)}, u32[]{:S(2)}) collective-permute-start(bf16[8,16,323]{2,1,0:T(8,128)(2,1)S(1)} %collective-permute-done.2), channel_id=1, source_target_pairs={{0,224},{8,232},{16,240},{24,248},{32,0},{40,8},{48,16},{56,24},{6... | collective-permute-start | bytes 248072 | tf_op jit(solution)/shard_map/ppermute | solution.py:41
  21.2 4.7 %collective-permute-start.6 = (bf16[8,16,323]{2,1,0:T(8,128)(2,1)S(1)}, bf16[8,16,323]{2,1,0:T(8,128)(2,1)S(1)}, u32[]{:S(2)}, u32[]{:S(2)}) collective-permute-start(bf16[8,16,323]{2,1,0:T(8,128)(2,1)S(1)} %collective-permute-done.5), channel_id=1, source_target_pairs={{0,32},{8,40},{16,48},{24,56},{32,64},{40,72},{48,80},{56,88},{64,... | collective-permute-start | bytes 248072 | tf_op jit(solution)/shard_map/ppermute | solution.py:41
  22.9 7.7 %collective-permute-start.4 = (bf16[8,16,323]{2,1,0:T(8,128)(2,1)S(1)}, bf16[8,16,323]{2,1,0:T(8,128)(2,1)S(1)}, u32[]{:S(2)}, u32[]{:S(2)}) collective-permute-start(bf16[8,16,323]{2,1,0:T(8,128)(2,1)S(1)} %collective-permute-done.3), channel_id=1, source_target_pairs={{0,224},{8,232},{16,240},{24,248},{32,0},{40,8},{48,16},{56,24},{6... | collective-permute-start | bytes 248072 | tf_op jit(solution)/shard_map/ppermute | solution.py:41
  25.9 4.7 %collective-permute-start.7 = (bf16[8,16,323]{2,1,0:T(8,128)(2,1)S(1)}, bf16[8,16,323]{2,1,0:T(8,128)(2,1)S(1)}, u32[]{:S(2)}, u32[]{:S(2)}) collective-permute-start(bf16[8,16,323]{2,1,0:T(8,128)(2,1)S(1)} %collective-permute-done.6), channel_id=1, source_target_pairs={{0,32},{8,40},{16,48},{24,56},{32,64},{40,72},{48,80},{56,88},{64,... | collective-permute-start | bytes 248072 | tf_op jit(solution)/shard_map/ppermute | solution.py:41
  30.6 4.9 %collective-permute-start.8 = (bf16[8,16,323]{2,1,0:T(8,128)(2,1)S(1)}, bf16[8,16,323]{2,1,0:T(8,128)(2,1)S(1)}, u32[]{:S(2)}, u32[]{:S(2)}) collective-permute-start(bf16[8,16,323]{2,1,0:T(8,128)(2,1)S(1)} %collective-permute-done.7), channel_id=1, source_target_pairs={{0,32},{8,40},{16,48},{24,56},{32,64},{40,72},{48,80},{56,88},{64,... | collective-permute-start | bytes 248072 | tf_op jit(solution)/shard_map/ppermute | solution.py:41
  37.2 1.0 copy-start.17
  39.0 1.3 copy-start.5
  40.3 17.1 %copy-start.16 = (bf16[1024,576]{0,1:T(8,128)(2,1)S(1)}, bf16[1024,576]{0,1:T(8,128)(2,1)}, u32[]{:S(2)}) copy-start(bf16[1024,576]{0,1:T(8,128)(2,1)} %param.10) | copy-start | bytes 3538948
  40.3 17.1 %copy-start.18 = (bf16[1024,576]{0,1:T(8,128)(2,1)S(1)}, bf16[1024,576]{0,1:T(8,128)(2,1)}, u32[]{:S(2)}) copy-start(bf16[1024,576]{0,1:T(8,128)(2,1)} %copy-done.17) | copy-start | bytes 3538948
  54.9 1.0 copy-start.10
  56.0 2.0 %copy-start = (bf16[2048,1024]{1,0:T(8,128)(2,1)}, bf16[2048,1024]{1,0:T(8,128)(2,1)S(1)}, u32[]{:S(2)}) copy-start(bf16[2048,1024]{1,0:T(8,128)(2,1)S(1)} %get-tuple-element.21.expo_ref) | copy-start | bytes 12582916
  56.0 20.7 %collective-permute-start.10 = (f32[3,1024]{1,0:T(4,128)S(1)}, f32[3,1024]{1,0:T(4,128)S(1)}, u32[]{:S(2)}, u32[]{:S(2)}) collective-permute-start(f32[3,1024]{1,0:T(4,128)S(1)} %get-tuple-element.22.own_ref), channel_id=1, source_target_pairs={{0,16},{8,24},{16,0},{24,8},{32,48},{40,56},{48,32},{56,40},{64,80... | collective-permute-start | bytes 36872 | tf_op jit(solution)/shard_map/ppermute | solution.py:41
  72.7 2.0 %copy-start.2 = (bf16[2048,1024]{1,0:T(8,128)(2,1)}, bf16[2048,1024]{1,0:T(8,128)(2,1)S(1)}, u32[]{:S(2)}) copy-start(bf16[2048,1024]{1,0:T(8,128)(2,1)S(1)} %get-tuple-element.20.spread_ref) | copy-start | bytes 12582916
  74.7 1.0 copy-start.12
  75.7 1.0 copy-start.14
  77.4 11.2 %all-to-all-start = ((f32[8,3,1024]{2,1,0:T(4,128)}), f32[8,3,1024]{2,1,0:T(4,128)S(1)}, u32[]{:S(2)}, u32[]{:S(2)}) async-start(f32[8,3,1024]{2,1,0:T(4,128)} %broadcast_in_dim.5), calls=%async_computation | async-start | bytes 262144 | tf_op jit(solution)/shard_map/all_to_all | solution.py:410
  88.7 2.2 %copy-start.3 = (bf16[2048,1024]{1,0:T(8,128)(2,1)S(1)}, bf16[2048,1024]{1,0:T(8,128)(2,1)}, u32[]{:S(2)}) copy-start(bf16[2048,1024]{1,0:T(8,128)(2,1)} %copy-done.2) | copy-start | bytes 12582916
  90.8 1.2 copy-start.11
  92.1 1.2 copy-start.13
  93.3 1.2 copy-start.15
  100.7 1.1 copy-start.6
  101.8 1.1 copy-start.8
  102.9 8.8 %copy-start.7 = (bf16[1024,576]{1,0:T(8,128)(2,1)S(1)}, bf16[1024,576]{1,0:T(8,128)(2,1)}, u32[]{:S(2)}) copy-start(bf16[1024,576]{1,0:T(8,128)(2,1)} %copy-done.6) | copy-start | bytes 3538948
  104.3 18.4 %collective-permute-start.11 = (bf16[1024,576]{0,1:T(8,128)(2,1)}, bf16[1024,576]{0,1:T(8,128)(2,1)}, u32[]{:S(2)}, u32[]{:S(2)}) collective-permute-start(bf16[1024,576]{0,1:T(8,128)(2,1)} %copy.121), channel_id=1, source_target_pairs={{0,8},{8,0},{16,24},{24,16},{32,40},{40,32},{48,56},{56,48},{64,72... | collective-permute-start | bytes 3538952 | tf_op jit(solution)/shard_map/ppermute | solution.py:41
  111.7 2.2 %copy-start.1 = (bf16[2048,1024]{1,0:T(8,128)(2,1)S(1)}, bf16[2048,1024]{1,0:T(8,128)(2,1)}, u32[]{:S(2)}) copy-start(bf16[2048,1024]{1,0:T(8,128)(2,1)} %copy-done) | copy-start | bytes 12582916
  113.8 2.2 %copy-start.4 = (bf16[2048,1024]{1,0:T(8,128)(2,1)S(1)}, bf16[2048,1024]{1,0:T(8,128)(2,1)}, u32[]{:S(2)}) copy-start(bf16[2048,1024]{1,0:T(8,128)(2,1)} %copy-done.2) | copy-start | bytes 12582916
  116.0 1.3 copy-start.9
  125.4 3.3 %copy-start.19 = (f32[2,1,128,576]{2,3,0,1:T(8,128)S(1)}, f32[2,1,128,576]{2,3,0,1:T(8,128)}, u32[]{:S(2)}) copy-start(f32[2,1,128,576]{2,3,0,1:T(8,128)} %copy.135) | copy-start | bytes 1769476
  130.3 17.6 %copy-start.20 = (bf16[2,1,128,576]{2,1,0,3:T(2,128)(2,1)S(1)}, bf16[2,1,128,576]{2,1,0,3:T(2,128)(2,1)}, u32[]{:S(2)}) copy-start(bf16[2,1,128,576]{2,1,0,3:T(2,128)(2,1)} %get-tuple-element.46) | copy-start | bytes 884740
  130.3 10.2 %collective-permute-start.14 = (bf16[2,128,576]{1,2,0:T(8,128)(2,1)}, bf16[2,128,576]{1,2,0:T(8,128)(2,1)S(1)}, u32[]{:S(2)}, u32[]{:S(2)}) collective-permute-start(bf16[2,128,576]{1,2,0:T(8,128)(2,1)} %get-tuple-element.35), channel_id=1, source_target_pairs={{0,1},{1,2},{2,3},{3,0},{4,5},{5,6},{6,7},{7,4},{8,9},{9,10},{10,1... | collective-permute-start | bytes 884744 | tf_op jit(solution)/shard_map/ppermute | solution.py:41
  131.6 16.3 %collective-permute-start.15 = (bf16[2,128,576]{1,2,0:T(8,128)(2,1)S(1)}, bf16[2,128,576]{1,2,0:T(8,128)(2,1)S(1)}, u32[]{:S(2)}, u32[]{:S(2)}) collective-permute-start(bf16[2,128,576]{1,2,0:T(8,128)(2,1)S(1)} %get-tuple-element.36), channel_id=1, source_target_pairs={{0,2},{1,3},{2,0},{3,1},{4,6},{5,7},{6,4},{7,5},{8,10},{9,11},{10,... | collective-permute-start | bytes 884744 | tf_op jit(solution)/shard_map/ppermute | solution.py:41
  134.2 13.7 %collective-permute-start.16 = (bf16[2,128,576]{1,2,0:T(8,128)(2,1)}, bf16[2,128,576]{1,2,0:T(8,128)(2,1)}, u32[]{:S(2)}, u32[]{:S(2)}) collective-permute-start(bf16[2,128,576]{1,2,0:T(8,128)(2,1)} %fusion.4), channel_id=1, source_target_pairs={{0,3},{1,0},{2,1},{3,2},{4,7},{5,4},{6,5},{7,6},{8,11},{9,8},{10,9... | collective-permute-start | bytes 884744 | tf_op jit(solution)/shard_map/ppermute | solution.py:41
  135.3 21.4 %all-to-all-start.1 = ((bf16[8,8,16,192]{3,2,1,0:T(8,128)(2,1)}), bf16[8,8,16,192]{3,2,1,0:T(8,128)(2,1)S(1)}, u32[]{:S(2)}, u32[]{:S(2)}) async-start(bf16[8,8,16,192]{3,2,1,0:T(8,128)(2,1)} %get-tuple-element.34), calls=%async_computation.1 | async-start | bytes 1048576 | tf_op jit(solution)/shard_map/all_to_all | solution.py:437
  149.1 12.3 %collective-permute-start.17 = (bf16[128,576]{0,1:T(8,128)(2,1)S(1)}, bf16[128,576]{0,1:T(8,128)(2,1)S(1)}, u32[]{:S(2)}, u32[]{:S(2)}) collective-permute-start(bf16[128,576]{0,1:T(8,128)(2,1)S(1)} %fusion.6), channel_id=1, source_target_pairs={{0,4},{1,5},{2,6},{3,7},{4,0},{5,1},{6,2},{7,3},{8,12},{9,13},{10,... | collective-permute-start | bytes 442376 | tf_op jit(solution)/shard_map/ppermute | solution.py:41
  156.8 2.9 %collective-permute-start.12 = (bf16[8,8,192]{2,0,1:T(8,128)(2,1)S(1)}, bf16[8,8,192]{2,0,1:T(8,128)(2,1)S(1)}, u32[]{:S(2)}, u32[]{:S(2)}) collective-permute-start(bf16[8,8,192]{2,0,1:T(8,128)(2,1)S(1)} %bitcast.116), channel_id=1, source_target_pairs={{0,16},{8,24},{16,0},{24,8},{32,48},{40,56},{48,32},{56,40},{64,80... | collective-permute-start | bytes 73736 | tf_op jit(solution)/shard_map/ppermute | solution.py:41
  159.7 2.6 %collective-permute-start.13 = (bf16[8,4,192]{2,0,1:T(8,128)(2,1)S(1)}, bf16[8,4,192]{2,0,1:T(8,128)(2,1)S(1)}, u32[]{:S(2)}, u32[]{:S(2)}) collective-permute-start(bf16[8,4,192]{2,0,1:T(8,128)(2,1)S(1)} %get-tuple-element.52), channel_id=1, source_target_pairs={{0,8},{8,0},{16,24},{24,16},{32,40},{40,32},{48,56},{56,48},{64,72... | collective-permute-start | bytes 36872 | tf_op jit(solution)/shard_map/ppermute | solution.py:41
where the time goes:
time: 164 us; the launch traced here: 163 us
  starting transfers between devices  40.8 us (25%)
  Pallas kernels  39.1 us (24%)
  local copies, waits for them, and re-layouts  37.5 us (23%)
  waiting for transfers between devices  36.1 us (22%)
  other arithmetic  7.63 us (5%)
  between operations  1.76 us (1%)
    ppermute x18, starting transfers between devices, permute(): lax.ppermute(x, axis, [(i, to(i)) for i in range(lax.axis_size(axis))])  34 us
    unnamed x61, local copies, waits for them, and re-layouts  25.8 us
    ppermute x18, waiting for transfers between devices, permute(): lax.ppermute(x, axis, [(i, to(i)) for i in range(lax.axis_size(axis))])  23.4 us
    pallas_call x1, Pallas kernels, project(): pl.pallas_call(project_kernel, out_shape=(jax.ShapeDtypeStruct((total, q_...  14.7 us
    pallas_call x1, Pallas kernels, attend(): pl.pallas_call(functools.partial(attend_kernel, score_scale), out_shape=(...  14.6 us
    all_to_all x1, waiting for transfers between devices, per_device(): lax.all_to_all(jnp.broadcast_to(joined[None], (nz,) + joined.shape), 'ctx...  7.7 us
    pallas_call x1, Pallas kernels, weigh(): pl.pallas_call(functools.partial(weigh_kernel, scale), out_shape=(dq, wei...  6.18 us
    all_to_all x1, waiting for transfers between devices, per_device(): dq = lax.all_to_all(dq, 'ctx', 0, 0, axis_index_groups=z_groups)  4.95 us
  transfers between devices with their start and end apart: 20, of which 11 were waited for; matrix products, arithmetic and copies ran while one was open for 6% of the time, Pallas kernels for 11%

commit v1 on v0

v1 whole, which is shorter than its diff:
```python
import functools

import jax
import jax.numpy as jnp
from jax import lax
from jax.experimental import pallas as pl
from jax.experimental.pallas import tpu as pltpu
from jax.sharding import PartitionSpec as P

BETA = 0.1
LOSS_SCALE = 2048.0
LOG2E = 1.4426950408889634
NEVER = -1e30
FLOOR = -1e29
F32 = jnp.float32
BF16 = jnp.bfloat16
CHUNK = 128
PACKED = 384
MIB = 1024 * 1024
ATTEND_MIB = 18
PROJECT_MIB = 12
WEIGH_MIB = 16
CACHE_MIB = 20


def permute(x, axis, to):
    return lax.ppermute(x, axis, [(i, to(i)) for i in range(lax.axis_size(axis))])


def in_order(mine, theirs, second, axis):
    return jnp.where(
        second,
        jnp.concatenate([theirs, mine], axis),
        jnp.concatenate([mine, theirs], axis),
    )


def pick(x, index, axis):
    first = lax.index_in_dim(x, 0, axis, keepdims=False)
    second = lax.index_in_dim(x, 1, axis, keepdims=False)
    return jnp.where(index == 1, second, first)


def join_stats(first, second):
    top = jnp.maximum(first[0:1], second[0:1])
    both = jnp.exp2(first[0:1] - top) * first + jnp.exp2(second[0:1] - top) * second
    return jnp.where(lax.broadcasted_iota(jnp.int32, both.shape, 0) == 0, top, both)


def join_kernel(first_ref, second_ref, out_ref):
    out_ref[...] = join_stats(first_ref[...], second_ref[...])


def join(first, second):
    vmem = pl.BlockSpec(memory_space=pltpu.VMEM)
    return pl.pallas_call(
        join_kernel,
        out_shape=jax.ShapeDtypeStruct(first.shape, F32),
        in_specs=[vmem, vmem],
        out_specs=vmem,
        compiler_params=pltpu.CompilerParams(vmem_limit_bytes=MIB),
    )(first, second)


def against(x, y):
    return lax.dot_general(x, y, (((1,), (1,)), ((), ())), preferred_element_type=F32)


def stage_kernel(where_ref, *refs):
    cache_ref, out_ref = refs[0], refs[len(refs) // 2]
    out_ref[...] = cache_ref[...].T
    if len(refs) == 4:
        refs[3][...] = refs[1][...]


def stage(where, cache_t, kv_up=None, steps=4):
    c_width, keys = cache_t.shape
    width = keys // steps
    out_shape = [jax.ShapeDtypeStruct((keys, c_width), BF16)]
    in_specs = [pl.BlockSpec((c_width, width), lambda p, w: (0, p))]
    out_specs = [pl.BlockSpec((width, c_width), lambda p, w: (p, 0))]
    operands = [cache_t]
    if kv_up is not None:
        half = kv_up.shape[0] // 2
        block = (half // steps,) + kv_up.shape[1:]
        out_shape.append(jax.ShapeDtypeStruct((half,) + kv_up.shape[1:], BF16))
        in_specs.append(pl.BlockSpec(block, lambda p, w: (w[0] * steps + p, 0, 0)))
        out_specs.append(pl.BlockSpec(block, lambda p, w: (p, 0, 0)))
        operands.append(kv_up)
    return pl.pallas_call(
        stage_kernel,
        out_shape=out_shape,
        grid_spec=pltpu.PrefetchScalarGridSpec(
            num_scalar_prefetch=1, grid=(steps,), in_specs=in_specs, out_specs=out_specs
        ),
        compiler_params=pltpu.CompilerParams(vmem_limit_bytes=8 * MIB),
        cost_estimate=pl.CostEstimate(
            flops=keys * c_width, bytes_accessed=4 * keys * c_width, transcendentals=0
        ),
    )(where, *operands)


def attend_kernel(score_scale, blocks, where_ref, *refs):
    ring_refs, refs = refs[:blocks], refs[blocks:]
    kv_ref, own_ref, other_ref, query_ref, grad_ref, expo_ref, spread_ref, stats_ref = refs[:8]
    ratio_ref, raw, scores, dprod = refs[8:]
    size = ring_refs[0].shape[0]
    rows, d_nope = size * blocks, kv_ref.shape[2] // 2
    d_lat = kv_ref.shape[1]
    d_rope = query_ref.shape[1] - d_lat
    keys = own_ref.shape[0]
    width = query_ref.shape[0]
    for k in range(blocks):
        first = pl.multiple_of(where_ref[4 + k] * size, size)
        raw[pl.ds(first, size), :] = ring_refs[k][...]
    for j in range(kv_ref.shape[0]):
        at = slice(j * rows, (j + 1) * rows)
        lane = j * PACKED
        lat = against(raw[:, lane : lane + d_nope], kv_ref[j, :, :d_nope])
        query_ref[at, :d_lat] = lat.astype(BF16)
        query_ref[at, d_lat:] = raw[:, lane + 2 * d_nope : lane + 2 * d_nope + d_rope]
        lat = against(raw[:, lane + d_nope : lane + 2 * d_nope], kv_ref[j, :, d_nope:])
        grad_ref[at, :] = lat.astype(BF16)
    terms = raw[:, 2 * d_nope : 3 * d_nope].astype(F32)
    lane = lax.broadcasted_iota(jnp.int32, terms.shape, 1)
    terms = jnp.where((lane >= d_rope) & (lane < d_rope + 3), terms, 0.0)
    ratio_ref[...] = jnp.broadcast_to(jnp.sum(terms, axis=1, keepdims=True), ratio_ref.shape)
    scores[:keys] = against(own_ref[...], query_ref[...])
    scores[keys:] = against(other_ref[...], query_ref[...])
    dprod[:keys] = against(own_ref[:, :d_lat], grad_ref[...])
    dprod[keys:] = against(other_ref[:, :d_lat], grad_ref[...])
    steps = 2 * keys // CHUNK

    def fold(x, join):
        return join(x.reshape(CHUNK // 8, 8, width), axis=0)

    def highest(i, top):
        at = pl.ds(pl.multiple_of(i * CHUNK, CHUNK), CHUNK)
        first = jnp.where(i * CHUNK < keys, where_ref[1], where_ref[2] - keys) + i * CHUNK
        key = first + lax.broadcasted_iota(jnp.int32, (CHUNK, width), 0)
        value = jnp.where(key < where_ref[3], scores[at, :] * score_scale, NEVER)
        scores[at, :] = value
        return jnp.maximum(top, fold(value, jnp.max))

    top = lax.fori_loop(0, steps, highest, jnp.full((8, width), FLOOR, F32), unroll=2)
    top = jnp.max(top, axis=0, keepdims=True)

    def sums(i, so_far):
        at = pl.ds(pl.multiple_of(i * CHUNK, CHUNK), CHUNK)
        value = jnp.exp2(scores[at, :] - top)
        scores[at, :] = value
        expo_ref[at, :] = value.astype(BF16)
        return (
            so_far[0] + fold(value, jnp.sum),
            so_far[1] + fold(value * dprod[at, :], jnp.sum),
        )

    zero = jnp.zeros((8, width), F32)
    mass, dsum = lax.fori_loop(0, steps, sums, (zero, zero), unroll=2)
    mass = jnp.sum(mass, axis=0, keepdims=True)
    dsum = jnp.sum(dsum, axis=0, keepdims=True)
    centre = dsum / jnp.maximum(mass, 1e-30)

    def spreads(i, carry):
        at = pl.ds(pl.multiple_of(i * CHUNK, CHUNK), CHUNK)
        spread_ref[at, :] = (scores[at, :] * (dprod[at, :] - centre)).astype(BF16)
        return carry

    lax.fori_loop(0, steps, spreads, 0, unroll=2)
    stats_ref[0:1] = top
    stats_ref[1:2] = mass
    stats_ref[2:3] = dsum


def attend(where, ring, kv_up, own, other, score_scale):
    blocks, (size, packed) = len(ring), ring[0].shape
    half = packed // PACKED
    rows = blocks * size
    d_lat = kv_up.shape[1]
    keys, c_width = own.shape
    total = half * rows
    width = 2 * rows
    whole = lambda p, w: (0, 0)
    column = lambda p, w: (0, p)
    return pl.pallas_call(
        functools.partial(attend_kernel, score_scale, blocks),
        out_shape=(
            jax.ShapeDtypeStruct((total, c_width), BF16),
            jax.ShapeDtypeStruct((total, d_lat), BF16),
            jax.ShapeDtypeStruct((2 * keys, total), BF16),
            jax.ShapeDtypeStruct((2 * keys, total), BF16),
            jax.ShapeDtypeStruct((3, total), F32),
            jax.ShapeDtypeStruct((rows, 128), F32),
        ),
        grid_spec=pltpu.PrefetchScalarGridSpec(
            num_scalar_prefetch=1,
            grid=(half // 2,),
            in_specs=[pl.BlockSpec((size, 2 * PACKED), column)] * blocks
            + [
                pl.BlockSpec((2,) + kv_up.shape[1:], lambda p, w: (p, 0, 0)),
                pl.BlockSpec((keys, c_width), whole),
                pl.BlockSpec((keys, c_width), whole),
            ],
            out_specs=[
                pl.BlockSpec((width, c_width), lambda p, w: (p, 0)),
                pl.BlockSpec((width, d_lat), lambda p, w: (p, 0)),
                pl.BlockSpec((2 * keys, width), column),
                pl.BlockSpec((2 * keys, width), column),
                pl.BlockSpec((3, width), column),
                pl.BlockSpec((rows, 128), whole),
            ],
            scratch_shapes=[
                pltpu.VMEM((rows, 2 * PACKED), BF16),
                pltpu.VMEM((2 * keys, width), F32),
                pltpu.VMEM((2 * keys, width), F32),
            ],
        ),
        compiler_params=pltpu.CompilerParams(vmem_limit_bytes=ATTEND_MIB * MIB),
        cost_estimate=pl.CostEstimate(
            flops=2 * 2 * keys * total * (c_width + d_lat),
            bytes_accessed=8 * keys * total,
            transcendentals=2 * keys * total,
        ),
    )(where, *ring, kv_up, own, other)


def project_kernel(
    where_ref, own_ref, other_ref, spread_ref, expo_ref, kv_ref, by_spread_ref, by_expo_ref
):
    d_lat = kv_ref.shape[1]
    d_nope = kv_ref.shape[2] // 2
    rows = spread_ref.shape[1] // kv_ref.shape[0]
    for terms_ref, out_ref in ((spread_ref, by_spread_ref), (expo_ref, by_expo_ref)):
        keys = own_ref.shape[1]
        full = jnp.dot(own_ref[...], terms_ref[:keys], preferred_element_type=F32)
        full = full + jnp.dot(other_ref[...], terms_ref[keys:], preferred_element_type=F32)
        for j in range(kv_ref.shape[0]):
            at = slice(j * rows, (j + 1) * rows)
            lat = full[:d_lat, at].astype(BF16)
            out_ref[at, :d_nope] = lax.dot_general(
                lat,
                kv_ref[j, :, :d_nope],
                (((0,), (0,)), ((), ())),
                preferred_element_type=F32,
            )
            out_ref[at, d_nope:] = full[d_lat:, at].T


def project(p, where, own_t, other_t, spread, expo, kv_up, half, q_width):
    c_width, keys = own_t.shape
    width = 2 * spread.shape[1] // half
    column = pl.BlockSpec((2 * keys, width), lambda i, w: (0, p))
    result = pl.BlockSpec((width, q_width), lambda i, w: (0, 0))
    return pl.pallas_call(
        project_kernel,
        out_shape=(jax.ShapeDtypeStruct((width, q_width), F32),) * 2,
        grid_spec=pltpu.PrefetchScalarGridSpec(
            num_scalar_prefetch=1,
            grid=(1,),
            in_specs=[
                pl.BlockSpec((c_width, keys), lambda i, w: (0, 0)),
                pl.BlockSpec((c_width, keys), lambda i, w: (0, 0)),
                column,
                column,
                pl.BlockSpec((2,) + kv_up.shape[1:], lambda i, w: (p, 0, 0)),
            ],
            out_specs=[result, result],
        ),
        compiler_params=pltpu.CompilerParams(vmem_limit_bytes=PROJECT_MIB * MIB),
        cost_estimate=pl.CostEstimate(
            flops=8 * keys * width * c_width, bytes_accessed=8 * keys * width, transcendentals=0
        ),
    )(where, own_t, other_t, spread, expo, kv_up)


def row_gains(where_ref, lens_ref, ratio_ref, rows_of_core):
    rows = ratio_ref.shape[0]
    place = lax.broadcasted_iota(jnp.int32, (rows, 1), 0)
    turn = place % (2 * rows_of_core) >= rows_of_core
    swapped = jnp.where(turn, place - rows_of_core, place + rows_of_core)
    place = jnp.where(where_ref[0] == 1, swapped, place)
    ratio = ratio_ref[:, 0:1]
    segments = lens_ref.shape[0]
    members = []
    first = jnp.int32(0)
    for k in range(segments):
        last = first + lens_ref[k]
        members.append((place >= first) & (place < last))
        first = last
    sums = [jnp.sum(jnp.where(m, ratio, 0.0), axis=0, keepdims=True) for m in members]
    gains = jnp.zeros((rows, 1), F32)
    for p in range(segments // 2):
        margin = BETA * (sums[2 * p] - sums[2 * p + 1])
        weight = LOSS_SCALE * BETA / (1.0 + jnp.exp(margin))
        gains = jnp.where(members[2 * p], -weight, gains)
        gains = jnp.where(members[2 * p + 1], weight, gains)
    return gains


def weigh_kernel(scale, rows_of_core, where_ref, lens_ref, *refs):
    (joined_ref, last_ref, own_ref, ratio_ref, query_ref, grad_ref) = refs[:6]
    by_spread_refs, by_expo_refs = refs[6:-4:2], refs[7:-4:2]
    dq_keep_ref, dq_send_ref, with_spread_ref, with_expo_ref = refs[-4:]
    total = query_ref.shape[0]
    d_lat = grad_ref.shape[1]
    rows = ratio_ref.shape[0]
    half = total // rows
    gains = row_gains(where_ref, lens_ref, ratio_ref, rows_of_core)
    joined = join_stats(joined_ref[...], last_ref[...])
    centre = own_ref[2:3] / jnp.maximum(own_ref[1:2], 1e-30)
    factor = jnp.exp2(own_ref[0:1] - joined[0:1]) / joined[1:2]
    shift = joined[2:3] / joined[1:2] - centre
    sublane = lax.broadcasted_iota(jnp.int32, (8, total), 0)
    both = jnp.where(sublane == 0, factor, shift).T
    blocks, size = dq_keep_ref.shape[0], dq_keep_ref.shape[2] // 2
    second = where_ref[4 + blocks] == 1
    for h in range(half):
        at = slice(h * rows, (h + 1) * rows)
        part = slice((h % 2) * rows, (h % 2 + 1) * rows)
        factor = both[at, 0:1] * gains
        shift = both[at, 1:2]
        scaled = scale * factor
        dq = by_spread_refs[h // 2][part, :] - shift * by_expo_refs[h // 2][part, :]
        dq = scaled * dq
        if h % 2:
            for b in range(blocks):
                pieces = []
                for x in range(2):
                    first = (2 * b + x) * size
                    at_x = slice(first, first + size)
                    pieces.append(jnp.concatenate([before[at_x], dq[at_x]], axis=0))
                dq_keep_ref[b, h // 2] = jnp.where(second, pieces[1], pieces[0]).astype(BF16)
                dq_send_ref[b, h // 2] = jnp.where(second, pieces[0], pieces[1]).astype(BF16)
        before = dq
        query = scaled * query_ref[at, :].astype(F32)
        with_spread_ref[at, :] = query.astype(BF16)
        moved = shift * query
        with_expo_ref[at, :d_lat] = (
            factor * grad_ref[at, :].astype(F32) - moved[:, :d_lat]
        ).astype(BF16)
        with_expo_ref[at, d_lat:] = (-moved[:, d_lat:]).astype(BF16)


def weigh(where, lens, joined, last, stats, ratio, query, grad, projected, scale, blocks, q_dev):
    total, c_width = query.shape
    rows = ratio.shape[0]
    q_width = projected[0].shape[1]
    half = total // rows
    smem = pl.BlockSpec(memory_space=pltpu.SMEM)
    vmem = pl.BlockSpec(memory_space=pltpu.VMEM)
    dq = jax.ShapeDtypeStruct((blocks, half // 2, rows // blocks, q_width), BF16)
    weight = jax.ShapeDtypeStruct((total, c_width), BF16)
    inputs = (joined, last, stats, ratio, query, grad, *projected)
    return pl.pallas_call(
        functools.partial(weigh_kernel, scale, q_dev),
        out_shape=(dq, dq, weight, weight),
        in_specs=[smem, smem] + [vmem] * len(inputs),
        out_specs=[vmem] * 4,
        compiler_params=pltpu.CompilerParams(vmem_limit_bytes=WEIGH_MIB * MIB),
        cost_estimate=pl.CostEstimate(
            flops=10 * total * c_width, bytes_accessed=8 * total * c_width, transcendentals=0
        ),
    )(where, lens, *inputs)


def cache_kernel(part, d_lat, order_ref, spread_ref, expo_ref, with_spread_ref, with_expo_ref, *refs):
    adds, outs = refs[:-2], refs[-2:]
    keys = spread_ref.shape[3]

    def gather(ref):
        blocks = [ref[part, x, order_ref[i]] for i in range(2) for x in range(2)]
        return jnp.concatenate(blocks, axis=0)

    out = jnp.dot(gather(spread_ref), with_spread_ref[...], preferred_element_type=F32)
    out = out + jnp.dot(gather(expo_ref), with_expo_ref[...], preferred_element_type=F32)
    rope = out.shape[1] - d_lat
    for i in range(4):
        first = (i % 2) * d_lat
        lat = slice(first, first + d_lat)
        first = 2 * d_lat + (i % 2) * rope
        tail = slice(first, first + rope)
        at = slice(i * keys, (i + 1) * keys)
        for lanes, value in ((lat, out[at, :d_lat]), (tail, out[at, d_lat:])):
            if adds:
                value = value + adds[i // 2][:, lanes].astype(F32)
            outs[i // 2][:, lanes] = value.astype(outs[i // 2].dtype)


def cache_terms(part, order, d_lat, spread, expo, with_spread, with_expo, dtypes, adds=()):
    total, c_width = with_spread.shape
    keys = spread.shape[3]
    smem = pl.BlockSpec(memory_space=pltpu.SMEM)
    vmem = pl.BlockSpec(memory_space=pltpu.VMEM)
    return pl.pallas_call(
        functools.partial(cache_kernel, part, d_lat),
        out_shape=[jax.ShapeDtypeStruct((keys, 2 * c_width), dtype) for dtype in dtypes],
        in_specs=[smem] + [vmem] * (4 + len(adds)),
        out_specs=[vmem, vmem],
        compiler_params=pltpu.CompilerParams(vmem_limit_bytes=CACHE_MIB * MIB),
        cost_estimate=pl.CostEstimate(
            flops=16 * keys * total * c_width,
            bytes_accessed=16 * keys * total,
            transcendentals=0,
        ),
    )(order, spread, expo, with_spread, with_expo, *adds)


def per_device(queries, out_grad, kv_up, latent_cache, token_ratio, pair_lens, prompt_len):
    ctx_index = lax.axis_index("ctx")
    head_index = lax.axis_index("head")
    core = ctx_index & 1
    x_lo = (ctx_index >> 1) & 1
    z = ctx_index >> 2
    nz = lax.axis_size("ctx") // 4
    ny = lax.axis_size("head") // 2
    y = head_index & (ny - 1)
    x_hi = (head_index >= ny).astype(jnp.int32)
    other_core = lambda i: i ^ 1
    other_x_lo = lambda i: i ^ 2
    z_groups = [[4 * k + j for k in range(nz)] for j in range(4)]

    q_dev, heads, q_width = queries.shape
    p_dev, c_width = latent_cache.shape
    d_lat = kv_up.shape[1]
    d_rope = c_width - d_lat
    d_nope = q_width - d_rope
    half = heads // 2
    scale = q_width ** (-0.5)

    where = [core, ctx_index * p_dev, (ctx_index ^ 1) * p_dev, prompt_len[0]]
    where = where + [(z + k) & (nz - 1) for k in range(nz)] + [x_lo]
    where = jnp.stack(where).astype(jnp.int32)
    own_t = latent_cache.T
    other_t = permute(latent_cache, "ctx", other_core).T
    own_keys, kv_half = stage(where, own_t, kv_up)
    (other_keys,) = stage(where, other_t)

    high = lax.reduce_precision(token_ratio, 8, 7)
    middle = lax.reduce_precision(token_ratio - high, 8, 7)
    low = token_ratio - high - middle
    terms = jnp.stack([high, middle, low], axis=1).astype(BF16)
    terms = jnp.broadcast_to(terms[:, None, :], (q_dev, heads, 3))
    own = jnp.concatenate(
        [queries[:, :, :d_nope], out_grad, queries[:, :, d_nope:], terms], axis=2
    )
    own = jnp.pad(own, ((0, 0), (0, 0), (0, PACKED - own.shape[2])))
    own = own.reshape(q_dev, 2, half * PACKED)
    block = jnp.concatenate(
        [pick(own, core, 1), permute(pick(own, 1 - core, 1), "ctx", other_core)], 0
    )
    block = in_order(block, permute(block, "ctx", other_x_lo), x_lo == 1, 0)
    up = down = block
    ring = [block] + [None] * (nz - 1)
    for k in range(1, nz // 2 + 1):
        up = permute(up, "ctx", lambda i: (i + 4) % (4 * nz))
        ring[nz - k] = up
        if k < nz // 2:
            down = permute(down, "ctx", lambda i: (i - 4) % (4 * nz))
            ring[k] = down

    query, grad, expo, spread, stats, ratio = attend(
        where, ring, kv_half, own_keys, other_keys, scale * LOG2E
    )

    joined = stats
    projected = []
    pairings = [other_x_lo] + [lambda i, k=k: i ^ (4 << k) for k in range(nz.bit_length() - 1)]
    for p, pairing in enumerate(pairings):
        if p:
            joined = join(joined, last)
        last = permute(joined, "ctx", pairing)
        if p < half // 2:
            terms = project(p, where, own_t, other_t, spread, expo, kv_half, half, q_width)
            last, *terms = lax.optimization_barrier((last, *terms))
            projected += terms
    dq_keep, dq_send, with_spread, with_expo = weigh(
        where, pair_lens, joined, last, stats, ratio, query, grad, projected, scale, nz, q_dev
    )
    dq_pair = permute(dq_send, "ctx", other_x_lo)
    steps = (2, 1, 3, 0)
    order = jnp.stack([(y + k) & (ny - 1) for k in steps]).astype(jnp.int32)
    keys = p_dev // (2 * ny)
    shape = (2, 2, ny, keys, spread.shape[1])
    operands = (d_lat, spread.reshape(shape), expo.reshape(shape), with_spread, with_expo)
    sends = [cache_terms(1, order[k : k + 2], *operands, (BF16, BF16)) for k in (0, 2)]
    adds = [[permute(x, "ctx", other_core) for x in send] for send in sends]
    blocks = cache_terms(0, order[:2], *operands, (BF16, BF16), adds[0])
    last_block, total = cache_terms(0, order[2:], *operands, (BF16, F32), adds[1])
    blocks = [*blocks, last_block]
    dq = (dq_keep.astype(F32) + dq_pair.astype(F32)).astype(BF16)
    last_block, dq = lax.optimization_barrier((last_block, dq))
    blocks[-1] = last_block
    arrived = [
        permute(block, "head", lambda i, k=k: (i // ny) * ny + (i + k) % ny)
        for block, k in zip(blocks, steps)
    ]

    for part in arrived:
        total = total + part.astype(F32)
    total = jnp.stack(
        [
            jnp.concatenate(
                [
                    total[:, i * d_lat : (i + 1) * d_lat],
                    total[:, 2 * d_lat + i * d_rope : 2 * d_lat + (i + 1) * d_rope],
                ],
                axis=1,
            )
            for i in range(2)
        ]
    )
    across = permute(
        pick(total, 1 - x_hi, 0).astype(BF16), "head", lambda i: (i + ny) % (2 * ny)
    )

    dq = lax.all_to_all(dq, "ctx", 0, 0, axis_index_groups=z_groups)
    dq = jnp.sum(dq.astype(F32), axis=0).astype(BF16).reshape(half, 2, q_dev, q_width)
    theirs = permute(dq[:, 1], "ctx", other_core)
    query_grad = jnp.transpose(in_order(dq[:, 0], theirs, core == 1, 0), (1, 0, 2))

    cache_grad = (pick(total, x_hi, 0) + across.astype(F32)).astype(BF16)
    return (query_grad, cache_grad)


def solution(mesh):
    placed = (
        P("ctx", "head", None),
        P("ctx", "head", None),
        P("head", None, None),
        P("ctx", None),
        P("ctx"),
        P(),
        P(),
    )
    return jax.shard_map(
        per_device,
        mesh=mesh,
        in_specs=placed,
        out_specs=(P("ctx", "head", None), P(("ctx", "head"), None)),
        check_vma=False,
    )
```

time: 164 us -> 117 us (0.71)
  local copies, waits for them, and re-layouts: 37.5 us -> 6.78 us
  waiting for transfers between devices: 36.1 us -> 19.4 us
  other arithmetic: 7.63 us -> 2.83 us
  Pallas kernels: 39.1 us -> 42.1 us
  starting transfers between devices: 40.8 us -> 43.8 us
    unnamed x61 -> x10, local copies, waits for them, and re-layouts: 25.8 us -> 4.88 us
    all_to_all x1 -> x0, waiting for transfers between devices: 7.7 us -> none  [per_device(): lax.all_to_all(jnp.broadcast_to(joined[None], (nz,) + joined.shape), 'ctx...]
    ppermute x18 -> x24, waiting for transfers between devices: 23.4 us -> 16.4 us  [permute(): lax.ppermute(x, axis, [(i, to(i)) for i in range(lax.axis_size(axis))])]
    ppermute x18 -> x24, starting transfers between devices: 34 us -> 39.2 us  [permute(): lax.ppermute(x, axis, [(i, to(i)) for i in range(lax.axis_size(axis))])]
    dynamic_slice x8 -> x0, local copies, waits for them, and re-layouts: 3.58 us -> none  [the longest x7 3.49 us: pick(): return lax.dynamic_index_in_dim(x, index, axis, keepdims=False)]
    all_to_all x1 -> x0, starting transfers between devices: 3.37 us -> none  [per_device(): lax.all_to_all(jnp.broadcast_to(joined[None], (nz,) + joined.shape), 'ctx...]
    pallas_call x4 -> x15, Pallas kernels: 39.1 us -> 42.1 us  [the longest x4 14.4 us: project(): pl.pallas_call(project_kernel, out_shape=(jax.ShapeDtypeStruct((width, q_...]
    reshape x3 -> x2, local copies, waits for them, and re-layouts: 2.95 us -> 0.04 us  [the longest x1 0.02 us: per_device(): own = own.reshape(q_dev, 2, half * PACKED)]
  transfers between devices with their start and end apart: 20 -> 25, of which waited for: 11 -> 10; matrix products, arithmetic and copies ran while one was open for 6% -> 5% of each run, Pallas kernels for 11% -> 23%
where the time goes in v1:
time: 117 us; the launch traced here: 116 us
  starting transfers between devices  43.8 us (37%)
  Pallas kernels  42.1 us (36%)
  waiting for transfers between devices  19.4 us (17%)
  local copies, waits for them, and re-layouts  6.78 us (6%)
  other arithmetic  2.83 us (2%)
  between operations  1.55 us (1%)
    ppermute x24, starting transfers between devices, permute(): lax.ppermute(x, axis, [(i, to(i)) for i in range(lax.axis_size(axis))])  39.2 us
    ppermute x24, waiting for transfers between devices, permute(): lax.ppermute(x, axis, [(i, to(i)) for i in range(lax.axis_size(axis))])  16.4 us
    pallas_call x4, Pallas kernels, project(): pl.pallas_call(project_kernel, out_shape=(jax.ShapeDtypeStruct((width, q_...  14.4 us
    pallas_call x1, Pallas kernels, attend(): pl.pallas_call(functools.partial(attend_kernel, score_scale, blocks), out...  13.6 us
    pallas_call x4, Pallas kernels, cache_terms(): pl.pallas_call(functools.partial(cache_kernel, part, d_lat), out_shape=[j...  9.64 us
    unnamed x10, local copies, waits for them, and re-layouts  4.88 us
    all_to_all x1, starting transfers between devices, per_device(): dq = lax.all_to_all(dq, 'ctx', 0, 0, axis_index_groups=z_groups)  4.68 us
    all_to_all x1, waiting for transfers between devices, per_device(): dq = lax.all_to_all(dq, 'ctx', 0, 0, axis_index_groups=z_groups)  2.94 us
  transfers between devices with their start and end apart: 25, of which 10 were waited for; matrix products, arithmetic and copies ran while one was open for 5% of the time, Pallas kernels for 23%

profile of v1, /device:TPU:1, one launch (start us, length us, event | category | flops | bytes accessed | tf_op | source)
XLA Modules:
  0.0 116.4 jit_solution(2514854632723113938)
XLA Ops:
  0.6 3.3 %collective-permute-start.9 = (bf16[1024,576]{0,1:T(8,128)(2,1)}, bf16[1024,576]{0,1:T(8,128)(2,1)S(1)}, u32[]{:S(2)}, u32[]{:S(2)}) collective-permute-start(bf16[1024,576]{0,1:T(8,128)(2,1)} %param.10), channel_id=1, source_target_pairs={{0,8},{8,0},{16,24},{24,16},{32,40},{40,32},{48,56},{56,48},{64,72... | collective-permute-start | bytes 3538952 | tf_op jit(solution)/shard_map/ppermute | solution.py:27
  4.0 0.7 slice.38
  4.7 0.7 slice.39
  5.4 0.7 fusion.8
  6.1 0.1 copy.11
  6.2 0.8 fusion.6
  7.0 0.1 fusion.14
  7.1 0.1 collective-permute-start
  7.2 1.2 %collective-permute-done = bf16[4,3072]{1,0:T(4,128)(2,1)S(1)} collective-permute-done((bf16[4,3072]{1,0:T(4,128)(2,1)S(1)}, bf16[4,3072]{1,0:T(4,128)(2,1)S(1)}, u32[]{:S(2)}, u32[]{:S(2)}) %collective-permute-start) | collective-permute-done | bytes 24608 | tf_op jit(solution)/shard_map/ppermute | solution.py:27
  8.4 0.1 collective-permute-start.1
  8.6 2.9 %collective-permute-done.1 = bf16[8,3072]{1,0:T(8,128)(2,1)S(1)} collective-permute-done((bf16[8,3072]{1,0:T(8,128)(2,1)S(1)}, bf16[8,3072]{1,0:T(8,128)(2,1)S(1)}, u32[]{:S(2)}, u32[]{:S(2)}) %collective-permute-start.1) | collective-permute-done | bytes 49184 | tf_op jit(solution)/shard_map/ppermute | solution.py:27
  11.5 0.1 maximum_select_fusion.refs_0_
  11.5 0.1 collective-permute-start.5
  11.6 3.9 %collective-permute-start.2 = (bf16[16,3072]{1,0:T(8,128)(2,1)S(1)}, bf16[16,3072]{1,0:T(8,128)(2,1)S(1)}, u32[]{:S(2)}, u32[]{:S(2)}) collective-permute-start(bf16[16,3072]{1,0:T(8,128)(2,1)S(1)} %maximum_select_fusion.refs_0_), channel_id=1, source_target_pairs={{0,224},{8,232},{16,240},{24,248},{32,0},{40,8},{48,16},{56,24},{6... | collective-permute-start | bytes 294920 | tf_op jit(solution)/shard_map/ppermute | solution.py:27
  15.5 1.9 %collective-permute-done.5.refs_7_ = bf16[16,3072]{1,0:T(8,128)(2,1)S(1)} collective-permute-done((bf16[16,3072]{1,0:T(8,128)(2,1)S(1)}, bf16[16,3072]{1,0:T(8,128)(2,1)S(1)}, u32[]{:S(2)}, u32[]{:S(2)}) %collective-permute-start.5) | collective-permute-done | bytes 98336 | tf_op jit(solution)/shard_map/ppermute | solution.py:27
  18.1 0.1 stack.83.where_ref
  18.2 1.3 %copy-done = bf16[1024,576]{0,1:T(8,128)(2,1)S(1)} copy-done((bf16[1024,576]{0,1:T(8,128)(2,1)S(1)}, bf16[1024,576]{0,1:T(8,128)(2,1)}, u32[]{:S(2)}) %copy-start) | copy-done | bytes 1179672
  19.5 2.2 %copy-done.2 = bf16[16,512,256]{2,1,0:T(8,128)(2,1)S(1)} copy-done((bf16[16,512,256]{2,1,0:T(8,128)(2,1)S(1)}, bf16[16,512,256]{2,1,0:T(8,128)(2,1)}, u32[]{:S(2)}) %copy-start.2) | copy-done | bytes 4194328
  21.7 1.3 %shard_map.86 = (bf16[1024,576]{1,0:T(8,128)(2,1)S(1)}, bf16[8,512,256]{2,1,0:T(8,128)(2,1)S(1)}) custom-call(s32[13]{0:T(128)S(1)} %stack.83.where_ref, bf16[576,1024]{1,0:T(8,128)(2,1)S(1)} %bitcast.46, bf16[16,512,256]{2,1,0:T(8,128)(2,1)S(1)} %copy-done.2), custom_call_target="tpu_custom_call" | custom-call | flops 589824 | bytes 2359296 | tf_op jit(solution)/shard_map/pallas_call | solution.py:90
  23.0 2.7 %collective-permute-start.3 = (bf16[16,3072]{1,0:T(8,128)(2,1)S(1)}, bf16[16,3072]{1,0:T(8,128)(2,1)S(1)}, u32[]{:S(2)}, u32[]{:S(2)}) collective-permute-start(bf16[16,3072]{1,0:T(8,128)(2,1)S(1)} %collective-permute-done.2.refs_1_), channel_id=1, source_target_pairs={{0,224},{8,232},{16,240},{24,248},{32,0},{40,8},{48,16},{56,24},{6... | collective-permute-start | bytes 294920 | tf_op jit(solution)/shard_map/ppermute | solution.py:27
  25.8 0.1 pad_add_fusion.1.order_ref
  25.8 1.6 %collective-permute-done.3.refs_2_ = bf16[16,3072]{1,0:T(8,128)(2,1)S(1)} collective-permute-done((bf16[16,3072]{1,0:T(8,128)(2,1)S(1)}, bf16[16,3072]{1,0:T(8,128)(2,1)S(1)}, u32[]{:S(2)}, u32[]{:S(2)}) %collective-permute-start.3) | collective-permute-done | bytes 98336 | tf_op jit(solution)/shard_map/ppermute | solution.py:27
  27.4 3.0 %collective-permute-start.4 = (bf16[16,3072]{1,0:T(8,128)(2,1)S(1)}, bf16[16,3072]{1,0:T(8,128)(2,1)S(1)}, u32[]{:S(2)}, u32[]{:S(2)}) collective-permute-start(bf16[16,3072]{1,0:T(8,128)(2,1)S(1)} %collective-permute-done.3.refs_2_), channel_id=1, source_target_pairs={{0,224},{8,232},{16,240},{24,248},{32,0},{40,8},{48,16},{56,24},{6... | collective-permute-start | bytes 294920 | tf_op jit(solution)/shard_map/ppermute | solution.py:27
  30.4 0.1 pad_add_fusion.order_ref
  30.5 1.3 %shard_map.87.refs_10_ = bf16[1024,576]{1,0:T(8,128)(2,1)S(1)} custom-call(s32[13]{0:T(128)S(1)} %stack.83.where_ref, bf16[576,1024]{1,0:T(8,128)(2,1)S(1)} %bitcast.51), custom_call_target="tpu_custom_call" | custom-call | flops 589824 | bytes 2359296 | tf_op jit(solution)/shard_map/pallas_call | solution.py:90
  31.8 0.2 collective-permute-done.4.refs_3_
  32.1 3.0 %collective-permute-done.8.refs_4_ = bf16[16,3072]{1,0:T(8,128)(2,1)S(1)} collective-permute-done((bf16[16,3072]{1,0:T(8,128)(2,1)S(1)}, bf16[16,3072]{1,0:T(8,128)(2,1)S(1)}, u32[]{:S(2)}, u32[]{:S(2)}) %collective-permute-start.8) | collective-permute-done | bytes 98336 | tf_op jit(solution)/shard_map/ppermute | solution.py:27
  35.1 13.6 %shard_map.88 = (bf16[1024,576]{1,0:T(8,128)(2,1)S(1)}, bf16[1024,512]{1,0:T(8,128)(2,1)S(1)}, bf16[2048,1024]{1,0:T(8,128)(2,1)S(1)}, bf16[2048,1024]{1,0:T(8,1...) custom-call(s32[13]{0:T(128)S(1)} %stack.83.where_ref, bf16[16,3072]{1,0:T(8,128)(2,1)S(1)} %maximum_select_fusion.refs_0_, ...), custom_call_target="tpu_custom_call" | custom-call | flops 4563402752 | bytes 8388608 | tf_op jit(solution)/shard_map/pallas_call | solution.py:185
  48.7 1.3 %collective-permute-start.10 = (f32[3,1024]{1,0:T(4,128)S(1)}, f32[3,1024]{1,0:T(4,128)S(1)}, u32[]{:S(2)}, u32[]{:S(2)}) collective-permute-start(f32[3,1024]{1,0:T(4,128)S(1)} %get-tuple-element.48.first_ref.refs_2_), channel_id=1, source_target_pairs={{0,16},{8,24},{16,0},{24,8},{32,48},{40,56},{48,32},{56,40},{64,80... | collective-permute-start | bytes 36872 | tf_op jit(solution)/shard_map/ppermute | solution.py:27
  50.0 3.6 %shard_map.89 = (f32[256,192]{1,0:T(8,128)S(1)}, f32[256,192]{1,0:T(8,128)S(1)}) custom-call(s32[13]{0:T(128)S(1)} %stack.83.where_ref, bf16[576,1024]{1,0:T(8,128)(2,1)S(1)} %bitcast.47, bf16[576,1024]{1,0:T(8,128)(2,1)S(1)} %bitcast.52, bf16[2048,1024]{1,0:T(8,128)(2,1)S(1)} %get-tuple-element.46.spread_ref, ...), custom_call_target="tpu_custom_call" | custom-call | flops 1207959552 | bytes 2097152 | tf_op jit(solution)/shard_map/pallas_call | solution.py:254
  53.7 0.3 collective-permute-start.11
  53.9 3.6 %shard_map.91 = (f32[256,192]{1,0:T(8,128)S(1)}, f32[256,192]{1,0:T(8,128)S(1)}) custom-call(s32[13]{0:T(128)S(1)} %stack.83.where_ref, bf16[576,1024]{1,0:T(8,128)(2,1)S(1)} %bitcast.48, bf16[576,1024]{1,0:T(8,128)(2,1)S(1)} %bitcast.53, bf16[2048,1024]{1,0:T(8,128)(2,1)S(1)} %get-tuple-element.46.spread_ref, ...), custom_call_target="tpu_custom_call" | custom-call | flops 1207959552 | bytes 2097152 | tf_op jit(solution)/shard_map/pallas_call | solution.py:254
  57.6 2.0 %collective-permute-start.12 = (f32[3,1024]{1,0:T(4,128)S(1)}, f32[3,1024]{1,0:T(4,128)S(1)}, u32[]{:S(2)}, u32[]{:S(2)}) collective-permute-start(f32[3,1024]{1,0:T(4,128)S(1)} %shard_map.92.first_ref), channel_id=1, source_target_pairs={{0,64},{8,72},{16,80},{24,88},{32,96},{40,104},{48,112},{56,120},{... | collective-permute-start | bytes 36872 | tf_op jit(solution)/shard_map/ppermute | solution.py:27
  59.6 3.6 %shard_map.93 = (f32[256,192]{1,0:T(8,128)S(1)}, f32[256,192]{1,0:T(8,128)S(1)}) custom-call(s32[13]{0:T(128)S(1)} %stack.83.where_ref, bf16[576,1024]{1,0:T(8,128)(2,1)S(1)} %bitcast.49, bf16[576,1024]{1,0:T(8,128)(2,1)S(1)} %bitcast.54, bf16[2048,1024]{1,0:T(8,128)(2,1)S(1)} %get-tuple-element.46.spread_ref, ...), custom_call_target="tpu_custom_call" | custom-call | flops 1207959552 | bytes 2097152 | tf_op jit(solution)/shard_map/pallas_call | solution.py:254
  63.2 0.0 copy-start.3
  63.2 2.2 %collective-permute-start.13 = (f32[3,1024]{1,0:T(4,128)S(1)}, f32[3,1024]{1,0:T(4,128)S(1)}, u32[]{:S(2)}, u32[]{:S(2)}) collective-permute-start(f32[3,1024]{1,0:T(4,128)S(1)} %shard_map.94.refs_0_), channel_id=1, source_target_pairs={{0,128},{8,136},{16,144},{24,152},{32,160},{40,168},{48,176},{56,1... | collective-permute-start | bytes 36872 | tf_op jit(solution)/shard_map/ppermute | solution.py:27
  65.5 3.6 %shard_map.95 = (f32[256,192]{1,0:T(8,128)S(1)}, f32[256,192]{1,0:T(8,128)S(1)}) custom-call(s32[13]{0:T(128)S(1)} %stack.83.where_ref, bf16[576,1024]{1,0:T(8,128)(2,1)S(1)} %bitcast.50, bf16[576,1024]{1,0:T(8,128)(2,1)S(1)} %bitcast.55, bf16[2048,1024]{1,0:T(8,128)(2,1)S(1)} %get-tuple-element.46.spread_ref, ...), custom_call_target="tpu_custom_call" | custom-call | flops 1207959552 | bytes 2097152 | tf_op jit(solution)/shard_map/pallas_call | solution.py:254
  69.1 0.7 collective-permute-done.13.refs_1_
  69.8 1.7 %shard_map.96 = (bf16[8,4,16,192]{3,2,1,0:T(8,128)(2,1)S(1)}, bf16[8,4,16,192]{3,2,1,0:T(8,128)(2,1)S(1)}, bf16[1024,576]{1,0:T(8,128)(2,1)S(1)}, bf16[1024,576]{1,0:T(8,128)(2,1)S(1)}) custom-call(s32[13]{0:T(128)S(1)} %stack.83.where_ref, s32[4]{0:T(128)S(1)} %copy-done.3, f32[3,1024]{1,0:T(4,128)S(1)} %shard_map.94.refs_0_, ...), custom_call_target="tpu_custom_call" | custom-call | flops 5898240 | bytes 4718592 | tf_op jit(solution)/shard_map/pallas_call | solution.py:354
  71.5 0.3 collective-permute-start.16
  71.9 2.4 %shard_map.99 = (bf16[128,1152]{1,0:T(8,128)(2,1)S(1)}, bf16[128,1152]{1,0:T(8,128)(2,1)S(1)}) custom-call(s32[2]{0:T(128)S(1)} %pad_add_fusion.1.order_ref, bf16[2,2,4,128,1024]{4,3,2,1,0:T(8,128)(2,1)S(1)} %bitcast.42, bf16[2,2,4,128,1024]{4,3,2,1,0:T(8,128)(2,1)S(1)} %bitcast.38, bf16[1024,576]{1,0:T(8,128)(2,1)S(1)} %get-tuple-element.72.with_spread_ref, ...), custom_call_target="tpu_custom_call" | custom-call | flops 1207959552 | bytes 2097152 | tf_op jit(solution)/shard_map/pallas_call | solution.py:394
  74.3 7.4 %collective-permute-start.18 = (bf16[128,1152]{1,0:T(8,128)(2,1)S(1)}, bf16[128,1152]{1,0:T(8,128)(2,1)S(1)}, u32[]{:S(2)}, u32[]{:S(2)}) collective-permute-start(bf16[128,1152]{1,0:T(8,128)(2,1)S(1)} %get-tuple-element.81), channel_id=1, source_target_pairs={{0,8},{8,0},{16,24},{24,16},{32,40},{40,32},{48,56},{56,48},{64,72... | collective-permute-start | bytes 884744 | tf_op jit(solution)/shard_map/ppermute | solution.py:27
  81.7 0.1 collective-permute-start.19
  81.8 2.4 %shard_map.97 = (bf16[128,1152]{1,0:T(8,128)(2,1)S(1)}, bf16[128,1152]{1,0:T(8,128)(2,1)S(1)}) custom-call(s32[2]{0:T(128)S(1)} %pad_add_fusion.order_ref, bf16[2,2,4,128,1024]{4,3,2,1,0:T(8,128)(2,1)S(1)} %bitcast.43, bf16[2,2,4,128,1024]{4,3,2,1,0:T(8,128)(2,1)S(1)} %bitcast.39, bf16[1024,576]{1,0:T(8,128)(2,1)S(1)} %get-tuple-element.72.with_spread_ref, ...), custom_call_target="tpu_custom_call" | custom-call | flops 1207959552 | bytes 2097152 | tf_op jit(solution)/shard_map/pallas_call | solution.py:394
  84.2 0.5 collective-permute-start.14
  84.7 0.3 collective-permute-start.15
  85.0 0.8 add_convert_fusion
  85.8 2.4 %shard_map.100 = (bf16[128,1152]{1,0:T(8,128)(2,1)S(1)}, bf16[128,1152]{1,0:T(8,128)(2,1)S(1)}) custom-call(s32[2]{0:T(128)S(1)} %pad_add_fusion.1.order_ref, bf16[2,2,4,128,1024]{4,3,2,1,0:T(8,128)(2,1)S(1)} %bitcast.44, bf16[2,2,4,128,1024]{4,3,2,1,0:T(8,128)(2,1)S(1)} %bitcast.40, bf16[1024,576]{1,0:T(8,128)(2,1)S(1)} %get-tuple-element.72.with_spread_ref, ...), custom_call_target="tpu_custom_call" | custom-call | flops 1207959552 | bytes 2097152 | tf_op jit(solution)/shard_map/pallas_call | solution.py:394
  88.2 3.0 %collective-permute-start.20 = (bf16[128,1152]{1,0:T(8,128)(2,1)S(1)}, bf16[128,1152]{1,0:T(8,128)(2,1)S(1)}, u32[]{:S(2)}, u32[]{:S(2)}) collective-permute-start(bf16[128,1152]{1,0:T(8,128)(2,1)S(1)} %get-tuple-element.83), channel_id=1, source_target_pairs={{0,2},{1,3},{2,0},{3,1},{4,6},{5,7},{6,4},{7,5},{8,10},{9,11},{10,... | collective-permute-start | bytes 884744 | tf_op jit(solution)/shard_map/ppermute | solution.py:27
  91.2 0.4 collective-permute-start.21
  91.6 2.4 %shard_map.98 = (bf16[128,1152]{1,0:T(8,128)(2,1)S(1)}, f32[128,1152]{1,0:T(8,128)S(1)}) custom-call(s32[2]{0:T(128)S(1)} %pad_add_fusion.order_ref, bf16[2,2,4,128,1024]{4,3,2,1,0:T(8,128)(2,1)S(1)} %bitcast.45, bf16[2,2,4,128,1024]{4,3,2,1,0:T(8,128)(2,1)S(1)} %bitcast.41, bf16[1024,576]{1,0:T(8,128)(2,1)S(1)} %get-tuple-element.72.with_spread_ref, ...), custom_call_target="tpu_custom_call" | custom-call | flops 1207959552 | bytes 2097152 | tf_op jit(solution)/shard_map/pallas_call | solution.py:394
  94.0 2.4 %collective-permute-start.22 = (bf16[128,1152]{1,0:T(8,128)(2,1)S(1)}, bf16[128,1152]{1,0:T(8,128)(2,1)S(1)}, u32[]{:S(2)}, u32[]{:S(2)}) collective-permute-start(bf16[128,1152]{1,0:T(8,128)(2,1)S(1)} %get-tuple-element.85), channel_id=1, source_target_pairs={{0,3},{1,0},{2,1},{3,2},{4,7},{5,4},{6,5},{7,6},{8,11},{9,8},{10,9... | collective-permute-start | bytes 884744 | tf_op jit(solution)/shard_map/ppermute | solution.py:27
  96.4 4.7 %all-to-all-start = ((bf16[8,4,16,192]{3,2,1,0:T(8,128)(2,1)}), bf16[8,4,16,192]{3,2,1,0:T(8,128)(2,1)S(1)}, u32[]{:S(2)}, u32[]{:S(2)}) async-start(bf16[8,4,16,192]{3,2,1,0:T(8,128)(2,1)} %add_convert_fusion), calls=%async_computation | async-start | bytes 524288 | tf_op jit(solution)/shard_map/all_to_all | solution.py:516
  101.1 4.0 %collective-permute-done.21 = bf16[128,1152]{1,0:T(8,128)(2,1)S(1)} collective-permute-done((bf16[128,1152]{1,0:T(8,128)(2,1)S(1)}, bf16[128,1152]{1,0:T(8,128)(2,1)S(1)}, u32[]{:S(2)}, u32[]{:S(2)}) %collective-permute-start.21) | collective-permute-done | bytes 294944 | tf_op jit(solution)/shard_map/ppermute | solution.py:27
  105.1 0.1 convert_add_fusion
  105.2 0.1 fusion.12
  105.2 0.1 fusion.13
  105.4 2.8 %collective-permute-start.23 = (bf16[128,576]{1,0:T(8,128)(2,1)S(1)}, bf16[128,576]{1,0:T(8,128)(2,1)S(1)}, u32[]{:S(2)}, u32[]{:S(2)}) collective-permute-start(bf16[128,576]{1,0:T(8,128)(2,1)S(1)} %select_convert_fusion), channel_id=1, source_target_pairs={{0,4},{1,5},{2,6},{3,7},{4,0},{5,1},{6,2},{7,3},{8,12},{9,13},{10,... | collective-permute-start | bytes 442376 | tf_op jit(solution)/shard_map/ppermute | solution.py:27
  108.2 2.9 %all-to-all-done = bf16[8,4,16,192]{3,2,1,0:T(8,128)(2,1)S(1)} async-done(((bf16[8,4,16,192]{3,2,1,0:T(8,128)(2,1)}), bf16[8,4,16,192]{3,2,1,0:T(8,128)(2,1)S(1)}, u32[]{:S(2)}, u32[]{:S(2)}) %all-to-all-start) | async-done | bytes 196640 | tf_op jit(solution)/shard_map/all_to_all | solution.py:516
  111.2 2.8 %collective-permute-start.17 = (bf16[8,4,192]{2,1,0:T(4,128)(2,1)S(1)}, bf16[8,4,192]{2,1,0:T(4,128)(2,1)S(1)}, u32[]{:S(2)}, u32[]{:S(2)}) collective-permute-start(bf16[8,4,192]{2,1,0:T(4,128)(2,1)S(1)} %get-tuple-element.98), channel_id=1, source_target_pairs={{0,8},{8,0},{16,24},{24,16},{32,40},{40,32},{48,56},{56,48},{64,72... | collective-permute-start | bytes 36872 | tf_op jit(solution)/shard_map/ppermute | solution.py:27
  114.1 0.8 collective-permute-done.17
  115.0 0.6 copy.15
  115.6 0.1 add_convert_fusion.1
  115.6 0.8 copy.16
  (36 shorter events, 0.4 us)
Async XLA Ops:
  0.6 29.9 %collective-permute-start.9 = (bf16[1024,576]{0,1:T(8,128)(2,1)}, bf16[1024,576]{0,1:T(8,128)(2,1)S(1)}, u32[]{:S(2)}, u32[]{:S(2)}) collective-permute-start(bf16[1024,576]{0,1:T(8,128)(2,1)} %param.10), channel_id=1, source_target_pairs={{0,8},{8,0},{16,24},{24,16},{32,40},{40,32},{48,56},{56,48},{64,72... | collective-permute-start | bytes 3538952 | tf_op jit(solution)/shard_map/ppermute | solution.py:27
  7.1 1.3 %collective-permute-start = (bf16[4,3072]{1,0:T(4,128)(2,1)S(1)}, bf16[4,3072]{1,0:T(4,128)(2,1)S(1)}, u32[]{:S(2)}, u32[]{:S(2)}) collective-permute-start(bf16[4,3072]{1,0:T(4,128)(2,1)S(1)} %get-tuple-element.95), channel_id=1, source_target_pairs={{0,8},{8,0},{16,24},{24,16},{32,40},{40,32},{48,56},{56,48},{64,72... | collective-permute-start | bytes 73736 | tf_op jit(solution)/shard_map/ppermute | solution.py:27
  8.4 3.0 %collective-permute-start.1 = (bf16[8,3072]{1,0:T(8,128)(2,1)S(1)}, bf16[8,3072]{1,0:T(8,128)(2,1)S(1)}, u32[]{:S(2)}, u32[]{:S(2)}) collective-permute-start(bf16[8,3072]{1,0:T(8,128)(2,1)S(1)} %pad_maximum_fusion.2), channel_id=1, source_target_pairs={{0,16},{8,24},{16,0},{24,8},{32,48},{40,56},{48,32},{56,40},{64,80... | collective-permute-start | bytes 147464 | tf_op jit(solution)/shard_map/ppermute | solution.py:27
  11.5 5.9 %collective-permute-start.5 = (bf16[16,3072]{1,0:T(8,128)(2,1)S(1)}, bf16[16,3072]{1,0:T(8,128)(2,1)S(1)}, u32[]{:S(2)}, u32[]{:S(2)}) collective-permute-start(bf16[16,3072]{1,0:T(8,128)(2,1)S(1)} %maximum_select_fusion.refs_0_), channel_id=1, source_target_pairs={{0,32},{8,40},{16,48},{24,56},{32,64},{40,72},{48,80},{56,88},{64,... | collective-permute-start | bytes 294920 | tf_op jit(solution)/shard_map/ppermute | solution.py:27
  11.6 11.4 %collective-permute-start.2 = (bf16[16,3072]{1,0:T(8,128)(2,1)S(1)}, bf16[16,3072]{1,0:T(8,128)(2,1)S(1)}, u32[]{:S(2)}, u32[]{:S(2)}) collective-permute-start(bf16[16,3072]{1,0:T(8,128)(2,1)S(1)} %maximum_select_fusion.refs_0_), channel_id=1, source_target_pairs={{0,224},{8,232},{16,240},{24,248},{32,0},{40,8},{48,16},{56,24},{6... | collective-permute-start | bytes 294920 | tf_op jit(solution)/shard_map/ppermute | solution.py:27
  17.5 8.3 %collective-permute-start.6 = (bf16[16,3072]{1,0:T(8,128)(2,1)S(1)}, bf16[16,3072]{1,0:T(8,128)(2,1)S(1)}, u32[]{:S(2)}, u32[]{:S(2)}) collective-permute-start(bf16[16,3072]{1,0:T(8,128)(2,1)S(1)} %collective-permute-done.5.refs_7_), channel_id=1, source_target_pairs={{0,32},{8,40},{16,48},{24,56},{32,64},{40,72},{48,80},{56,88},{64,... | collective-permute-start | bytes 294920 | tf_op jit(solution)/shard_map/ppermute | solution.py:27
  18.2 1.3 %copy-start = (bf16[1024,576]{0,1:T(8,128)(2,1)S(1)}, bf16[1024,576]{0,1:T(8,128)(2,1)}, u32[]{:S(2)}) copy-start(bf16[1024,576]{0,1:T(8,128)(2,1)} %param.10) | copy-start | bytes 3538948
  19.5 2.2 %copy-start.2 = (bf16[16,512,256]{2,1,0:T(8,128)(2,1)S(1)}, bf16[16,512,256]{2,1,0:T(8,128)(2,1)}, u32[]{:S(2)}) copy-start(bf16[16,512,256]{2,1,0:T(8,128)(2,1)} %refs_1_.1) | copy-start | bytes 12582916
  23.0 4.4 %collective-permute-start.3 = (bf16[16,3072]{1,0:T(8,128)(2,1)S(1)}, bf16[16,3072]{1,0:T(8,128)(2,1)S(1)}, u32[]{:S(2)}, u32[]{:S(2)}) collective-permute-start(bf16[16,3072]{1,0:T(8,128)(2,1)S(1)} %collective-permute-done.2.refs_1_), channel_id=1, source_target_pairs={{0,224},{8,232},{16,240},{24,248},{32,0},{40,8},{48,16},{56,24},{6... | collective-permute-start | bytes 294920 | tf_op jit(solution)/shard_map/ppermute | solution.py:27
  25.8 4.7 %collective-permute-start.7 = (bf16[16,3072]{1,0:T(8,128)(2,1)S(1)}, bf16[16,3072]{1,0:T(8,128)(2,1)S(1)}, u32[]{:S(2)}, u32[]{:S(2)}) collective-permute-start(bf16[16,3072]{1,0:T(8,128)(2,1)S(1)} %collective-permute-done.6.refs_6_), channel_id=1, source_target_pairs={{0,32},{8,40},{16,48},{24,56},{32,64},{40,72},{48,80},{56,88},{64,... | collective-permute-start | bytes 294920 | tf_op jit(solution)/shard_map/ppermute | solution.py:27
  27.4 4.7 %collective-permute-start.4 = (bf16[16,3072]{1,0:T(8,128)(2,1)S(1)}, bf16[16,3072]{1,0:T(8,128)(2,1)S(1)}, u32[]{:S(2)}, u32[]{:S(2)}) collective-permute-start(bf16[16,3072]{1,0:T(8,128)(2,1)S(1)} %collective-permute-done.3.refs_2_), channel_id=1, source_target_pairs={{0,224},{8,232},{16,240},{24,248},{32,0},{40,8},{48,16},{56,24},{6... | collective-permute-start | bytes 294920 | tf_op jit(solution)/shard_map/ppermute | solution.py:27
  30.4 4.7 %collective-permute-start.8 = (bf16[16,3072]{1,0:T(8,128)(2,1)S(1)}, bf16[16,3072]{1,0:T(8,128)(2,1)S(1)}, u32[]{:S(2)}, u32[]{:S(2)}) collective-permute-start(bf16[16,3072]{1,0:T(8,128)(2,1)S(1)} %collective-permute-done.7.refs_5_), channel_id=1, source_target_pairs={{0,32},{8,40},{16,48},{24,56},{32,64},{40,72},{48,80},{56,88},{64,... | collective-permute-start | bytes 294920 | tf_op jit(solution)/shard_map/ppermute | solution.py:27
  35.1 14.9 %copy-start.1 = (bf16[1024,576]{0,1:T(8,128)(2,1)S(1)}, bf16[1024,576]{0,1:T(8,128)(2,1)}, u32[]{:S(2)}) copy-start(bf16[1024,576]{0,1:T(8,128)(2,1)} %param.10) | copy-start | bytes 3538948
  48.7 4.9 %collective-permute-start.10 = (f32[3,1024]{1,0:T(4,128)S(1)}, f32[3,1024]{1,0:T(4,128)S(1)}, u32[]{:S(2)}, u32[]{:S(2)}) collective-permute-start(f32[3,1024]{1,0:T(4,128)S(1)} %get-tuple-element.48.first_ref.refs_2_), channel_id=1, source_target_pairs={{0,16},{8,24},{16,0},{24,8},{32,48},{40,56},{48,32},{56,40},{64,80... | collective-permute-start | bytes 36872 | tf_op jit(solution)/shard_map/ppermute | solution.py:27
  53.7 3.9 %collective-permute-start.11 = (f32[3,1024]{1,0:T(4,128)S(1)}, f32[3,1024]{1,0:T(4,128)S(1)}, u32[]{:S(2)}, u32[]{:S(2)}) collective-permute-start(f32[3,1024]{1,0:T(4,128)S(1)} %shard_map.90.first_ref), channel_id=1, source_target_pairs={{0,32},{8,40},{16,48},{24,56},{32,0},{40,8},{48,16},{56,24},{64,96... | collective-permute-start | bytes 36872 | tf_op jit(solution)/shard_map/ppermute | solution.py:27
  57.6 5.6 %collective-permute-start.12 = (f32[3,1024]{1,0:T(4,128)S(1)}, f32[3,1024]{1,0:T(4,128)S(1)}, u32[]{:S(2)}, u32[]{:S(2)}) collective-permute-start(f32[3,1024]{1,0:T(4,128)S(1)} %shard_map.92.first_ref), channel_id=1, source_target_pairs={{0,64},{8,72},{16,80},{24,88},{32,96},{40,104},{48,112},{56,120},{... | collective-permute-start | bytes 36872 | tf_op jit(solution)/shard_map/ppermute | solution.py:27
  63.2 6.6 %copy-start.3 = (s32[4]{0:T(128)S(1)}, s32[4]{0:T(128)}, u32[]{:S(2)}) copy-start(s32[4]{0:T(128)} %lens_ref.1) | copy-start | bytes 52
  63.2 6.6 %collective-permute-start.13 = (f32[3,1024]{1,0:T(4,128)S(1)}, f32[3,1024]{1,0:T(4,128)S(1)}, u32[]{:S(2)}, u32[]{:S(2)}) collective-permute-start(f32[3,1024]{1,0:T(4,128)S(1)} %shard_map.94.refs_0_), channel_id=1, source_target_pairs={{0,128},{8,136},{16,144},{24,152},{32,160},{40,168},{48,176},{56,1... | collective-permute-start | bytes 36872 | tf_op jit(solution)/shard_map/ppermute | solution.py:27
  71.5 13.5 %collective-permute-start.16 = (bf16[8,4,16,192]{3,2,1,0:T(8,128)(2,1)S(1)}, bf16[8,4,16,192]{3,2,1,0:T(8,128)(2,1)S(1)}, u32[]{:S(2)}, u32[]{:S(2)}) collective-permute-start(bf16[8,4,16,192]{3,2,1,0:T(8,128)(2,1)S(1)} %get-tuple-element.78), channel_id=1, source_target_pairs={{0,16},{8,24},{16,0},{24,8},{32,48},{40,56},{48,32},{56,40},{64,80... | collective-permute-start | bytes 589832 | tf_op jit(solution)/shard_map/ppermute | solution.py:27
  74.3 11.5 %collective-permute-start.18 = (bf16[128,1152]{1,0:T(8,128)(2,1)S(1)}, bf16[128,1152]{1,0:T(8,128)(2,1)S(1)}, u32[]{:S(2)}, u32[]{:S(2)}) collective-permute-start(bf16[128,1152]{1,0:T(8,128)(2,1)S(1)} %get-tuple-element.81), channel_id=1, source_target_pairs={{0,8},{8,0},{16,24},{24,16},{32,40},{40,32},{48,56},{56,48},{64,72... | collective-permute-start | bytes 884744 | tf_op jit(solution)/shard_map/ppermute | solution.py:27
  81.7 4.1 %collective-permute-start.19 = (bf16[128,1152]{1,0:T(8,128)(2,1)S(1)}, bf16[128,1152]{1,0:T(8,128)(2,1)S(1)}, u32[]{:S(2)}, u32[]{:S(2)}) collective-permute-start(bf16[128,1152]{1,0:T(8,128)(2,1)S(1)} %get-tuple-element.82), channel_id=1, source_target_pairs={{0,8},{8,0},{16,24},{24,16},{32,40},{40,32},{48,56},{56,48},{64,72... | collective-permute-start | bytes 884744 | tf_op jit(solution)/shard_map/ppermute | solution.py:27
  84.2 7.4 %collective-permute-start.14 = (bf16[128,1152]{1,0:T(8,128)(2,1)S(1)}, bf16[128,1152]{1,0:T(8,128)(2,1)S(1)}, u32[]{:S(2)}, u32[]{:S(2)}) collective-permute-start(bf16[128,1152]{1,0:T(8,128)(2,1)S(1)} %get-tuple-element.74), channel_id=1, source_target_pairs={{0,8},{8,0},{16,24},{24,16},{32,40},{40,32},{48,56},{56,48},{64,72... | collective-permute-start | bytes 884744 | tf_op jit(solution)/shard_map/ppermute | solution.py:27
  84.7 6.9 %collective-permute-start.15 = (bf16[128,1152]{1,0:T(8,128)(2,1)S(1)}, bf16[128,1152]{1,0:T(8,128)(2,1)S(1)}, u32[]{:S(2)}, u32[]{:S(2)}) collective-permute-start(bf16[128,1152]{1,0:T(8,128)(2,1)S(1)} %get-tuple-element.75), channel_id=1, source_target_pairs={{0,8},{8,0},{16,24},{24,16},{32,40},{40,32},{48,56},{56,48},{64,72... | collective-permute-start | bytes 884744 | tf_op jit(solution)/shard_map/ppermute | solution.py:27
  88.2 12.9 %collective-permute-start.20 = (bf16[128,1152]{1,0:T(8,128)(2,1)S(1)}, bf16[128,1152]{1,0:T(8,128)(2,1)S(1)}, u32[]{:S(2)}, u32[]{:S(2)}) collective-permute-start(bf16[128,1152]{1,0:T(8,128)(2,1)S(1)} %get-tuple-element.83), channel_id=1, source_target_pairs={{0,2},{1,3},{2,0},{3,1},{4,6},{5,7},{6,4},{7,5},{8,10},{9,11},{10,... | collective-permute-start | bytes 884744 | tf_op jit(solution)/shard_map/ppermute | solution.py:27
  91.2 13.8 %collective-permute-start.21 = (bf16[128,1152]{1,0:T(8,128)(2,1)S(1)}, bf16[128,1152]{1,0:T(8,128)(2,1)S(1)}, u32[]{:S(2)}, u32[]{:S(2)}) collective-permute-start(bf16[128,1152]{1,0:T(8,128)(2,1)S(1)} %get-tuple-element.84), channel_id=1, source_target_pairs={{0,1},{1,2},{2,3},{3,0},{4,5},{5,6},{6,7},{7,4},{8,9},{9,10},{10,1... | collective-permute-start | bytes 884744 | tf_op jit(solution)/shard_map/ppermute | solution.py:27
  94.0 11.0 %collective-permute-start.22 = (bf16[128,1152]{1,0:T(8,128)(2,1)S(1)}, bf16[128,1152]{1,0:T(8,128)(2,1)S(1)}, u32[]{:S(2)}, u32[]{:S(2)}) collective-permute-start(bf16[128,1152]{1,0:T(8,128)(2,1)S(1)} %get-tuple-element.85), channel_id=1, source_target_pairs={{0,3},{1,0},{2,1},{3,2},{4,7},{5,4},{6,5},{7,6},{8,11},{9,8},{10,9... | collective-permute-start | bytes 884744 | tf_op jit(solution)/shard_map/ppermute | solution.py:27
  96.4 14.8 %all-to-all-start = ((bf16[8,4,16,192]{3,2,1,0:T(8,128)(2,1)}), bf16[8,4,16,192]{3,2,1,0:T(8,128)(2,1)S(1)}, u32[]{:S(2)}, u32[]{:S(2)}) async-start(bf16[8,4,16,192]{3,2,1,0:T(8,128)(2,1)} %add_convert_fusion), calls=%async_computation | async-start | bytes 524288 | tf_op jit(solution)/shard_map/all_to_all | solution.py:516
  105.4 10.2 %collective-permute-start.23 = (bf16[128,576]{1,0:T(8,128)(2,1)S(1)}, bf16[128,576]{1,0:T(8,128)(2,1)S(1)}, u32[]{:S(2)}, u32[]{:S(2)}) collective-permute-start(bf16[128,576]{1,0:T(8,128)(2,1)S(1)} %select_convert_fusion), channel_id=1, source_target_pairs={{0,4},{1,5},{2,6},{3,7},{4,0},{5,1},{6,2},{7,3},{8,12},{9,13},{10,... | collective-permute-start | bytes 442376 | tf_op jit(solution)/shard_map/ppermute | solution.py:27
  111.2 3.7 %collective-permute-start.17 = (bf16[8,4,192]{2,1,0:T(4,128)(2,1)S(1)}, bf16[8,4,192]{2,1,0:T(4,128)(2,1)S(1)}, u32[]{:S(2)}, u32[]{:S(2)}) collective-permute-start(bf16[8,4,192]{2,1,0:T(4,128)(2,1)S(1)} %get-tuple-element.98), channel_id=1, source_target_pairs={{0,8},{8,0},{16,24},{24,16},{32,40},{40,32},{48,56},{56,48},{64,72... | collective-permute-start | bytes 36872 | tf_op jit(solution)/shard_map/ppermute | solution.py:27
